TPU v7x, 32 devices: a whole 2x2x4 slice. The times are simulated.
32 devices in a mesh: expert: 8 (over z, core), seq: 4 (over y, x).
Axes of the slice: x: 2, y: 2, z: 4, core: 2. Of those that a mesh axis runs over, the one named last changes fastest.
Arguments:
- tokens: bfloat16 [8192, 1024], P(('expert', 'seq')), may hold values from -45 to 45
- cotangent: bfloat16 [8192, 1024], P(('expert', 'seq')), may hold values from -6 to 6
- expert_ids: int32 [8192, 2], P(('expert', 'seq')), may hold values from 0 to 7, all different within a row; in each aligned block of 256 rows (0 to 255, 256 to 511, ...) at most 160 rows name the same one
- segment_lengths: int32 [8, 13], P('expert'), may hold values from 1 to 409, 1024 in all within a row
- segment_parents: int32 [8, 13], P('expert'), may hold values from 0 to 11, as said below
- attention_gain: bfloat16 [1024], P(('expert', 'seq')), may hold values from 0.5 to 1.5
- query_weight: bfloat16 [1024, 1024], P(('expert', 'seq')), may hold values from -0.1875 to 0.1875
- key_weight: bfloat16 [1024, 1024], P(('expert', 'seq')), may hold values from -0.1875 to 0.1875
- value_weight: bfloat16 [1024, 1024], P(('expert', 'seq')), may hold values from -0.1875 to 0.1875
- output_weight: bfloat16 [1024, 1024], P(('expert', 'seq')), may hold values from -0.75 to 0.75
- bias_table: bfloat16 [512], P(('expert', 'seq')), may hold values from -4 to 4
- feedforward_gain: bfloat16 [1024], P(('expert', 'seq')), may hold values from 0.5 to 1.5
- router_weight: bfloat16 [1024, 8], P(('expert', 'seq')), may hold values from -0.1875 to 0.1875
- gate_weight: bfloat16 [8, 2816, 1024], P('expert', 'seq'), may hold values from -0.1875 to 0.1875
- up_weight: bfloat16 [8, 2816, 1024], P('expert', 'seq'), may hold values from -0.1875 to 0.1875
- down_weight: bfloat16 [8, 2816, 1024], P('expert', 'seq'), may hold values from -0.21875 to 0.21875
Outputs:
- layer_out: bfloat16 [8192, 1024], P(('expert', 'seq'))
- tokens_grad: float32 [8192, 1024], P(('expert', 'seq'))
- attention_gain_grad: float32 [1024], P(('expert', 'seq'))
- query_grad: float32 [1024, 1024], P(('expert', 'seq'))
- key_grad: float32 [1024, 1024], P(('expert', 'seq'))
- value_grad: float32 [1024, 1024], P(('expert', 'seq'))
- output_grad: float32 [1024, 1024], P(('expert', 'seq'))
- bias_table_grad: float32 [512], P(('expert', 'seq'))
- feedforward_gain_grad: float32 [1024], P(('expert', 'seq'))
- router_grad: float32 [1024, 8], P(('expert', 'seq'))
- gate_grad: float32 [8, 2816, 1024], P('expert', 'seq')
- up_grad: float32 [8, 2816, 1024], P('expert', 'seq')
- down_grad: float32 [8, 2816, 1024], P('expert', 'seq')
- root_mean_squares: float32 [2], replicated
Inputs may be any that keep to these rules, and one draw needn't show every extreme that they name: `expert_ids`: the two ids of a token differ. In the rows of one device no expert is named more than 2 * 80 times. `segment_lengths`: each tree's lengths sum to 1024. `segment_parents`: segment 0 is the root and its own parent; every other segment has a parent with a lower number; the last segment's parent is the one before it.
All inputs are finite; a program needn't handle non-finite values.
Results may differ from a plain program's by a relative error of at most 0.025.
Values may be sent and summed in bfloat16 or wider, within the bound.
A program may use at most 256 MiB of HBM per device.

v0:
```python
import math

import jax
import jax.numpy as jnp
from jax import lax
from jax.experimental import pallas as pl
from jax.experimental.pallas import tpu as pltpu
from jax.sharding import PartitionSpec as P

SPEC_0 = "qkb,bh->hqk"
SPEC_1 = "qhd,khd->hqk"
SPEC_2 = "hqk,khd->qhd"
SPEC_3 = "rd,fd->rf"
SPEC_4 = "rf,rd->fd"
SPEC_5 = "rd,re->de"
SPEC_6 = "re,de->rd"
SPEC_7 = "qkb,hqk->bh"
SPEC_8 = "hqk,qhd->khd"
MESH = pl.DeviceIdType.MESH
VMEM_LIMIT = 62 << 20
EXPERT, SEQ = "expert", "seq"
BOTH = (EXPERT, SEQ)

D = 1024
HEADS = 16
HDIM = 64
BUCKETS = 32
MAXDIST = 128


EPSILON = 1e-06
NEGATIVE = -1e30


def norm_factor(values):
    return lax.rsqrt(jnp.mean(values * values, axis=-1, keepdims=True) + EPSILON)


def gelu_tanh(values):
    return jax.nn.gelu(values, approximate=True)


def bucket_of(distance):
    exact_span = BUCKETS // 2
    above = jnp.zeros(distance.shape, jnp.int32)
    for number in range(exact_span):
        threshold = int(math.ceil(exact_span * (MAXDIST / exact_span) ** (number / exact_span)))
        above = above + (distance >= threshold).astype(jnp.int32)
    return jnp.where(distance < exact_span, distance, exact_span - 1 + above)


def tree_tables(lengths, parents):
    ordinal = jnp.arange(lengths.shape[0], dtype=jnp.int32)
    starts = jnp.cumsum(lengths) - lengths

    def chase(number, running):
        current, reaches = running
        current = jnp.sum(
            jnp.where(current[:, None] == ordinal[None, :], parents[None, :], 0), axis=1
        )
        reaches = jnp.maximum(reaches, (current[:, None] == ordinal[None, :]).astype(jnp.int32))
        return (current, reaches)

    begin = (ordinal, (ordinal[:, None] == ordinal[None, :]).astype(jnp.int32))
    unused, reaches = lax.fori_loop(0, lengths.shape[0], chase, begin)
    before = jnp.sum(reaches * lengths[None, :], axis=1) - lengths
    return (starts, before, reaches)


def token_info(token_rows, starts, before, reaches):
    ordinal = jnp.arange(starts.shape[0], dtype=jnp.int32)
    segment = jnp.sum((token_rows[:, None] >= starts[None, :]).astype(jnp.int32), axis=1) - 1
    member = segment[:, None] == ordinal[None, :]
    position = token_rows + jnp.sum(jnp.where(member, (before - starts)[None, :], 0), axis=1)
    lineage = jnp.sum(jnp.where(member[:, :, None], reaches[None, :, :], 0), axis=1)
    return (member.astype(jnp.float32), position, lineage.astype(jnp.float32))


def pair_terms(query_meta, key_meta, query_rows, key_rows, bias_grid):
    visible = jnp.dot(query_meta[2], key_meta[0].T, preferred_element_type=jnp.float32) > 0.5
    visible = visible & (key_rows[None, :] <= query_rows[:, None])
    distance = jnp.maximum(query_meta[1][:, None] - key_meta[1][None, :], 0)
    onehot = (
        bucket_of(distance)[:, :, None] == jnp.arange(BUCKETS, dtype=jnp.int32)[None, None, :]
    ).astype(jnp.bfloat16)
    pair_bias = jnp.einsum(SPEC_0, onehot, bias_grid, preferred_element_type=jnp.float32)
    return (visible, onehot, pair_bias)


def masked_scores(query_block, key_block, visible, pair_bias):
    scores = (
        jnp.einsum(SPEC_1, query_block, key_block, preferred_element_type=jnp.float32)
        * HDIM ** (-0.5)
        + pair_bias
    )
    return jnp.where(visible[None], scores, NEGATIVE)


def remote(src, dst, send, recv, peer):
    return pltpu.make_async_remote_copy(
        src_ref=src, dst_ref=dst, send_sem=send, recv_sem=recv,
        device_id=peer, device_id_type=MESH,
    )


def contract(left, right, dims):
    return lax.dot_general(left, right, (dims, ((), ())), preferred_element_type=jnp.float32)


def gelu_parts(values):
    root = 0.7978845608028654
    square = values * values
    swing = jnp.tanh(root * values * (1.0 + 0.044715 * square))
    half = 0.5 * (1.0 + swing)
    slope = half + 0.5 * values * (1.0 - swing * swing) * (root * (1.0 + 3 * 0.044715 * square))
    return values * half, slope


ORDER = (0, 1, 2, 3, 4, 5, 6, 7)
UNITS = (
    (0, 0), (0, 1), (1, 0), (2, 0), (3, 0), (1, 1), (2, 1), (3, 1),
    (0, 2), (1, 2), (2, 2), (0, 3), (3, 2), (1, 3), (2, 3), (3, 3),
)


def greet(peers):
    barrier = pltpu.get_barrier_semaphore()
    for peer in peers:
        pl.semaphore_signal(barrier, inc=1, device_id=peer, device_id_type=MESH)
    pl.semaphore_wait(barrier, len(peers))


def aligned(index, size):
    return pl.ds(pl.multiple_of(index * size, size), size)


ZHOPS = (2, 4, 6)


def expert_kernel(
    xs, gs, shares, g_early, wg_far, wu_far, wd_far, po_far, ret_b, ret_s, dwg, dwu, dwd,
    xr, gr, sh, act, gb, ub, po, pb, rb, rb2, sd, sd_got, sd_out, stage, rounded, wg, wu, wd,
    in_send, in_recv, hop_send, hop_recv, sh_send, sh_recv, rs_send, rs_recv, out_send, out_recv,
    sd_send, sd_recv, sr_send, sr_recv, po_sem, stage_sem, load_sem, own_sem,
):
    e = lax.axis_index(EXPERT)
    s = lax.axis_index(SEQ)
    cap = xs.shape[0] // 8
    width = xs.shape[1]
    full, low = jnp.float32, jnp.bfloat16
    near_x, near_y = (e, s ^ 1), (e, s ^ 2)
    around = (near_x, near_y, (e, s ^ 3))
    loads = [
        pltpu.make_async_copy(src, dst, load_sem.at[k])
        for k, (src, dst) in enumerate(((wg_far, wg), (wu_far, wu), (wd_far, wd), (g_early, gr.at[:, pl.ds(0, 4)])))
    ]
    for load in loads:
        load.start()
    greet(list(around) + [(e ^ d, s) for d in range(1, 8)])

    def block(index):
        return pl.ds(pl.multiple_of(index * cap, 16), cap)

    tensors = ((xs, xr), (gs, gr))

    def entry(kind, place):
        src, dst = tensors[kind]
        d = ORDER[place]
        return remote(src.at[block(e ^ d)], dst.at[0, place], in_send.at[kind, place],
                      in_recv.at[kind, place], (e ^ d, s))

    def hop(kind, which, pair):
        buf = tensors[kind][1]
        places = pl.ds(2 * pair, 2) if which < 2 else pl.ds(2 * pair + which - 2, 1)
        src = buf.at[(0, 0, 1, 2)[which], places]
        dst = buf.at[(1, 2, 3, 3)[which], places]
        peer = (near_x, near_y, near_y, near_x)[which]
        return remote(src, dst, hop_send.at[kind, which, pair], hop_recv.at[kind, which, pair], peer)

    def share_entry(place):
        d = ORDER[place]
        return remote(shares.at[e ^ d], sh.at[0, place], sh_send.at[place], sh_recv.at[place], (e ^ d, s))

    def share_hop(which):
        return remote(sh.at[(0, 0, 1)[which]], sh.at[1 + which], sh_send.at[8 + which], sh_recv.at[8 + which],
                      (near_x, near_y, near_y)[which])

    def rs(half, which, pair):
        first, second = ((near_x, near_y), (near_y, near_x))[half]
        src = pb.at[(1 + half, 3, 2 - half)[which], half, pair]
        dst = rb2.at[half, pair] if which == 2 else rb.at[which, half, pair]
        return remote(src, dst, rs_send.at[half, which, pair], rs_recv.at[half, which, pair],
                      second if which == 2 else first)

    def back(place):
        return remote(pb.at[0, place % 2, place // 2], ret_b.at[block(e)],
                      out_send.at[place], out_recv.at[place], (e ^ ORDER[place], s))

    def own_back():
        return pltpu.make_async_copy(pb.at[0, 0, 0], ret_b.at[block(e)], own_sem.at[2])

    def start_entries(kind, pair):
        for place in (2 * pair, 2 * pair + 1):
            if ORDER[place]:
                entry(kind, place).start()

    def forward_pair(kind, pair):
        for place in (2 * pair, 2 * pair + 1):
            if ORDER[place]:
                entry(kind, place).wait_recv()
        hop(kind, 0, pair).start()
        hop(kind, 1, pair).start()

    def forward_corner(kind, pair):
        for which in range(2):
            hop(kind, which, pair).wait_recv()
            hop(kind, 2 + which, pair).start()

    def wait_corner(pair):
        for kind in range(2 if pair >= 2 else 1):
            for which in (2, 3):
                hop(kind, which, pair).wait_recv()

    def start_sums(pair):
        for which in (1, 0):
            for half in range(2):
                rs(half, which, pair).start()

    def add_second(pair):
        for half in range(2):
            rs(half, 1, pair).wait_recv()
            group = 2 - half
            pb[group, half, pair] = (pb[group, half, pair].astype(full) + rb[1, half, pair].astype(full)).astype(low)
            rs(half, 2, pair).start()

    def finish(pair):
        for half in range(2):
            rs(half, 0, pair).wait_recv()
            rs(half, 2, pair).wait_recv()
            pb[0, half, pair] = (
                pb[0, half, pair].astype(full) + rb[0, half, pair].astype(full) + rb2[half, pair].astype(full)
            ).astype(low)
            if ORDER[2 * pair + half]:
                back(2 * pair + half).start()
            else:
                own_back().start()

    own_rows = [
        pltpu.make_async_copy(xs.at[block(e)], xr.at[0, 0], own_sem.at[0]),
        pltpu.make_async_copy(shares.at[e], sh.at[0, 0], own_sem.at[1]),
    ]
    for copy in own_rows:
        copy.start()
    start_entries(0, 0)
    for place in range(1, 8):
        share_entry(place).start()
    start_entries(0, 1)
    start_entries(1, 2)

    rows = 2 * cap

    def put_out(u, q, c):
        return pltpu.make_async_copy(po.at[q, :, c], po_far.at[q, :, c], po_sem.at[u])

    def unit(u, carry):
        q, c = jnp.int32(0), jnp.int32(0)
        for k, (whose, pair) in enumerate(UNITS):
            q, c = jnp.where(u == k, whose, q), jnp.where(u == k, pair, c)

        for k, (whose, pair) in enumerate(UNITS):
            @pl.when(u == k)
            def _():
                if k == 0:
                    for copy in own_rows:
                        copy.wait()
                    forward_pair(0, 0)
                    for place in range(1, 8):
                        share_entry(place).wait_recv()
                    share_hop(0).start()
                    share_hop(1).start()
                    for load in loads:
                        load.wait()
                if k == 1:
                    forward_corner(0, 0)
                    forward_pair(0, 1)
                    start_entries(1, 3)
                if k == 2:
                    share_hop(0).wait_recv()
                    share_hop(2).start()
                    share_hop(1).wait_recv()
                if k == 3:
                    forward_corner(0, 1)
                    forward_pair(1, 2)
                    start_entries(0, 2)
                if k == 4:
                    share_hop(2).wait_recv()
                if k == 6:
                    forward_corner(1, 2)
                    forward_pair(1, 3)
                    start_entries(0, 3)
                if k == 8:
                    forward_corner(1, 3)
                    forward_pair(0, 2)
                if k == 9:
                    forward_corner(0, 2)
                if k == 10:
                    add_second(1)
                if k == 11:
                    forward_pair(0, 3)
                if k == 13:
                    forward_corner(0, 3)
                    finish(1)
                if k == 15:
                    add_second(2)
                if whose == 3:
                    wait_corner(pair)

        x = xr[q, pl.ds(2 * c, 2)].reshape(rows, width)
        g = gr[q, pl.ds(2 * c, 2)].reshape(rows, width)
        share = jnp.concatenate([jnp.transpose(sh[q, 2 * c + i])[0:cap, 0:1] for i in range(2)], axis=0)
        gate = contract(x, wg[...], ((1,), (1,)))
        up = contract(x, wu[...], ((1,), (1,)))
        ag = contract(g, wd[...], ((1,), (1,))) * share
        value, slope = gelu_parts(gate)
        active = value * up
        gate_back = (ag * up * slope).astype(low)
        up_back = (ag * value).astype(low)
        act[q, c] = (active * share).astype(low)
        gb[q, c] = gate_back
        ub[q, c] = up_back
        out = contract(active.astype(low), wd[...], ((1,), (0,)))
        dots = lax.dot_general(jnp.ones((8, width), full), out * g.astype(full), (((1,), (1,)), ((), ())),
                               precision=lax.Precision.HIGHEST, preferred_element_type=full)
        sd[q, c, :, 0:rows] = dots
        weighted = (out * share).astype(low)
        into = contract(gate_back, wg[...], ((1,), (0,))) + contract(up_back, wu[...], ((1,), (0,)))
        for half in range(2):
            po[q, half, c] = weighted[half * cap:(half + 1) * cap]
            pb[q, half, c] = into[half * cap:(half + 1) * cap].astype(low)
        put_out(u, q, c).start()

        for k, (whose, pair) in enumerate(UNITS):
            if whose == 3 and pair:
                @pl.when(u == k)
                def _():
                    start_sums(pair)
            elif pair == 3 and whose:
                @pl.when(u == k)
                def _():
                    give_dots(whose).start()
        return carry

    def give_dots(q):
        return remote(sd.at[q], sd_got.at[q - 1], sd_send.at[q - 1], sd_recv.at[q - 1], around[q - 1])

    def return_dots(place):
        return remote(sd_out.at[place], ret_s.at[e], sr_send.at[place], sr_recv.at[place], (e ^ ORDER[place], s))

    def own_dots():
        return pltpu.make_async_copy(sd_out.at[0], ret_s.at[e], own_sem.at[3])

    sd[...] = jnp.zeros_like(sd)
    lax.fori_loop(0, len(UNITS), unit, 0)
    give_dots(3).start()

    def grads(left, right, dst):
        def part(u):
            q, c = lax.rem(u, 4), u // 4
            return contract(left[q, pl.ds(2 * c, 2)].reshape(2 * rows, wg.shape[0]),
                            right[q, pl.ds(4 * c, 4)].reshape(2 * rows, width), ((0,), (0,)))

        def more(u, carry):
            stage[...] += part(u)
            return carry

        stage[...] = part(0)
        lax.fori_loop(1, 8, more, 0)
        rounded[...] = stage[...].astype(low)
        done = pltpu.make_async_copy(rounded, dst, stage_sem)
        done.start()
        return done

    done = grads(gb, xr, dwg)
    finish(2)
    add_second(3)
    start_sums(0)
    for q in range(1, 4):
        give_dots(q).wait_recv()
    for c in range(4):
        dots = sd[0, c] + sd_got[0, c] + sd_got[1, c] + sd_got[2, c]
        for i in range(2):
            sd_out[2 * c + i] = jnp.zeros((8, 128), full)
            sd_out[2 * c + i, :, 0:cap] = dots[:, i * cap:(i + 1) * cap]
    for place in range(1, 8):
        return_dots(place).start()
    own_dots().start()
    done.wait()
    done = grads(ub, xr, dwu)
    finish(3)
    add_second(0)
    done.wait()
    done = grads(act, gr, dwd)
    finish(0)
    done.wait()

    own_back().wait()
    own_dots().wait()
    for place in range(1, 8):
        back(place).wait()
        return_dots(place).wait()
        share_entry(place).wait_send()
        for kind in range(2 if place >= 4 else 1):
            entry(kind, place).wait_send()
    for which in range(3):
        share_hop(which).wait_send()
        give_dots(1 + which).wait_send()
    for pair in range(4):
        for kind in range(2 if pair >= 2 else 1):
            for which in range(4):
                hop(kind, which, pair).wait_send()
        for half in range(2):
            for which in range(3):
                rs(half, which, pair).wait_send()
    for k, (whose, pair) in enumerate(UNITS):
        put_out(k, whose, pair).wait()


def experts(send_rows, grad_rows, shares, g_early, gate_weight, up_weight, down_weight):
    rows, width = send_rows.shape
    units = gate_weight.shape[0]
    cap = rows // 8
    low, full = jnp.bfloat16, jnp.float32
    hbm = pl.BlockSpec(memory_space=pl.ANY)
    dma = pltpu.SemaphoreType.DMA
    part = (4, 2, 4, cap, width)
    return pl.pallas_call(
        expert_kernel,
        out_shape=(
            jax.ShapeDtypeStruct(part, low),
            jax.ShapeDtypeStruct((rows, width), low),
            jax.ShapeDtypeStruct((8, 8, 128), full),
        ) + (jax.ShapeDtypeStruct((units, width), low),) * 3,
        in_specs=[hbm] * 7,
        out_specs=(hbm,) * 6,
        scratch_shapes=[
            pltpu.VMEM((4, 8, cap, width), low),
            pltpu.VMEM((4, 8, cap, width), low),
            pltpu.VMEM((4, 8, 8, 128), full),
            pltpu.VMEM((4, 4, 2 * cap, units), low),
            pltpu.VMEM((4, 4, 2 * cap, units), low),
            pltpu.VMEM((4, 4, 2 * cap, units), low),
            pltpu.VMEM(part, low),
            pltpu.VMEM(part, low),
            pltpu.VMEM((2, 2, 4, cap, width), low),
            pltpu.VMEM((2, 4, cap, width), low),
            pltpu.VMEM((4, 4, 8, 256), full),
            pltpu.VMEM((3, 4, 8, 256), full),
            pltpu.VMEM((8, 8, 128), full),
            pltpu.VMEM((units, width), full),
            pltpu.VMEM((units, width), low),
            pltpu.VMEM((units, width), low),
            pltpu.VMEM((units, width), low),
            pltpu.VMEM((units, width), low),
            dma((2, 8)), dma((2, 8)),
            dma((2, 4, 4)), dma((2, 4, 4)),
            dma((11,)), dma((11,)),
            dma((2, 3, 4)), dma((2, 3, 4)),
            dma((8,)), dma((8,)),
            dma((3,)), dma((3,)),
            dma((8,)), dma((8,)),
            dma((len(UNITS),)), dma, dma((4,)), dma((4,)),
        ],
        compiler_params=pltpu.CompilerParams(
            collective_id=1, has_side_effects=True, vmem_limit_bytes=VMEM_LIMIT
        ),
        cost_estimate=pl.CostEstimate(flops=2 * 9 * 4 * rows * units * width, bytes_accessed=20 << 20, transcendentals=4 * rows * units),
        name="experts",
    )(send_rows, grad_rows, shares, g_early, gate_weight, up_weight, down_weight)


def segment_scalars(lengths, parents, before_mem, reach_mem):
    count = lengths.shape[1]
    start = jnp.int32(0)
    found = []
    for k in range(count):
        length = lengths[0, k]
        if k == 0:
            before, reach = jnp.int32(0), jnp.int32(1)
        else:
            parent = parents[0, k]
            before = before_mem[parent] + lengths[0, parent]
            reach = reach_mem[parent] | (1 << k)
        before_mem[k] = before
        reach_mem[k] = reach
        found.append((start, before, reach, length))
        start = start + length
    return found


def token_columns(found, ids):
    offset = jnp.zeros(ids.shape, jnp.int32)
    reach = jnp.full(ids.shape, 1, jnp.int32)
    own = jnp.full(ids.shape, 1, jnp.int32)
    for k, (start, before, bits, _) in enumerate(found):
        if k:
            after = ids >= start
            offset = jnp.where(after, before - start, offset)
            reach = jnp.where(after, bits, reach)
            own = jnp.where(after, 1 << k, own)
    return ids + offset, reach, own


LAST = 127


def bias_tables(params, s):
    flat = params[2:3, 0:BUCKETS * HEADS]
    lane = lax.broadcasted_iota(jnp.int32, (8, BUCKETS * HEADS), 1)
    head = lax.broadcasted_iota(jnp.int32, (8, BUCKETS * HEADS), 0)
    heads_here = HEADS // 4
    chosen = jnp.where((lane % HEADS) == s * heads_here + head, jnp.broadcast_to(flat, lane.shape), 0.0)
    entry = lax.broadcasted_iota(jnp.int32, (BUCKETS * HEADS, LAST + 1), 0) // HEADS
    distance = lax.broadcasted_iota(jnp.int32, (BUCKETS * HEADS, LAST + 1), 1)
    hot = jnp.where(entry == bucket_of(distance), 1.0, 0.0)
    table = contract(chosen.astype(jnp.bfloat16), hot.astype(jnp.bfloat16), ((1,), (0,)))
    spot = lax.broadcasted_iota(jnp.int32, table.shape, 1)
    return jnp.where(spot == LAST, NEGATIVE, table)


def pair_index(found, first, rows, count):
    ids = first + lax.broadcasted_iota(jnp.int32, (rows, 1), 0)
    keys = lax.broadcasted_iota(jnp.int32, (1, count), 1)
    place, reach, _ = token_columns(found, ids)
    key_place, _, key_own = token_columns(found, keys)
    seen = ((reach & key_own) != 0) & (keys <= ids)
    return jnp.where(seen, jnp.minimum(place - key_place, LAST - 1), LAST), place, reach


def looked_up(row, index):
    rows, count = index.shape
    table = jnp.broadcast_to(row, (rows, LAST + 1))
    pieces = [
        jnp.take_along_axis(table, index[:, k * 128:(k + 1) * 128], axis=1)
        for k in range(count // 128)
    ]
    return jnp.concatenate(pieces, axis=1)


def slots_of(ids_row, cap):
    rows = ids_row.shape[1]
    full, low = jnp.float32, jnp.bfloat16
    level = lax.broadcasted_iota(jnp.int32, (8, rows), 0)
    hot_row = [jnp.where(ids_row[k:k + 1] == level, 1.0, 0.0).astype(full) for k in range(2)]
    down = lax.broadcasted_iota(jnp.int32, (rows, rows), 0)
    across = lax.broadcasted_iota(jnp.int32, (rows, rows), 1)
    after = jnp.where(down < across, 1.0, 0.0).astype(low)
    earlier = contract((hot_row[0] + hot_row[1]).astype(low), after, ((1,), (0,)))
    slot_row = [jnp.sum(h * earlier, axis=0, keepdims=True) for h in hot_row]
    spot_row = [
        jnp.where(slot_row[k] < cap, ids_row[k:k + 1].astype(full) * cap + slot_row[k], -1.0) for k in range(2)
    ]
    columns = jnp.transpose(jnp.concatenate(spot_row + slot_row + [jnp.zeros((4, rows), full)], axis=0))
    target = [columns[:, k:k + 1].astype(jnp.int32) for k in range(2)]
    slot = [columns[:, 2 + k:3 + k].astype(jnp.int32) for k in range(2)]
    hot = [jnp.transpose(h) for h in hot_row]
    target_row = [spot.astype(jnp.int32) for spot in spot_row]
    return hot_row, hot, slot, target, target_row


def router_of(residual, params, hot):
    low = jnp.bfloat16
    scale = norm_factor(residual)
    unit = residual * scale
    normed = (unit * params[1:2]).astype(low)
    router = params[8:16]
    logits = contract(normed, router.astype(low), ((1,), (1,)))
    expo = jnp.exp(logits - jnp.max(logits, axis=1, keepdims=True))
    prob = expo / jnp.sum(expo, axis=1, keepdims=True)
    chosen = [jnp.sum(h * prob, axis=1, keepdims=True) for h in hot]
    chosen_sum = chosen[0] + chosen[1]
    shares = [c / chosen_sum for c in chosen]
    return scale, unit, normed, router, prob, chosen_sum, shares


def front_kernel(
    lengths, parents, tokens, cotangent, ids_row, wq, wk, wv, wo, gain_one, gain_two, bias, router_row,
    xs, gs_far, shares, residual, all_tokens_far, qkv_far, cols_far, params, att_far, stats_far, wo_far, g_far,
    all_tokens, qkv, cols, wo_full, att, stats, got, part, normed, misc, tags, tag_sum, all_tags, index, table, landed, gs, g_early,
    before_mem, reach_mem,
    t_send, t_recv, w_send, w_recv, m_send, m_recv, c_send, c_recv, n_send, n_recv,
    h_send, h_recv, a_send, a_recv,
    e_send, e_recv, j_send, j_recv, far_sem,
):
    e, s = lax.axis_index(EXPERT), lax.axis_index(SEQ)
    near_x, near_y, corner = (e, s ^ 1), (e, s ^ 2), (e, s ^ 3)
    around = (near_x, near_y, corner)
    hops = (1,) + ZHOPS
    low, full = jnp.bfloat16, jnp.float32
    rows, width = tokens.shape
    slim = wq.shape[0]
    shard = width // 4
    weights = (wq, wk, wv)
    place = e * 4 + s

    at_gain = lax.broadcasted_iota(jnp.int32, (slim, width), 1) == place * slim + lax.broadcasted_iota(
        jnp.int32, (slim, width), 0)
    gain_spot = jnp.where(at_gain, 1.0, 0.0).astype(low)
    few = bias.shape[1]
    at_bias = lax.broadcasted_iota(jnp.int32, (few, width), 1) == place * few + lax.broadcasted_iota(
        jnp.int32, (few, width), 0)
    bias_spot = jnp.where(at_bias, 1.0, 0.0).astype(low)
    two_gains = [contract(one[...], gain_spot, ((1,), (0,))) for one in (gain_one, gain_two)]
    one_bias = contract(bias[...], bias_spot, ((1,), (0,)))
    misc[...] = jnp.concatenate(
        two_gains + [one_bias, jnp.zeros((5, width), full), contract(router_row[...], gain_spot, ((1,), (0,)))], axis=0
    ).astype(low)

    greet(list(around) + [(e ^ d, s) for d in (1, 2, 3, 4, 6)])

    def send_tokens(k):
        return remote(tokens, all_tokens.at[aligned(s, rows)], t_send.at[k], t_recv.at[k], around[k])

    def pass_tokens(k):
        piece = pl.ds(pl.multiple_of((s ^ (1 + k)) * rows + k * (rows // 2), rows // 2), rows // 2)
        view = all_tokens.at[piece]
        return remote(view, view, t_send.at[2 + k], t_recv.at[2 + k], around[1 - k])

    def send_cols(k, m):
        return remote(
            weights[m].at[:, aligned(s ^ (k + 1), shard)], got.at[m, aligned(s, slim)],
            w_send.at[k, m], w_recv.at[k, m], around[k],
        )

    def send_tags(k):
        return remote(misc, tags.at[k], m_send.at[k], m_recv.at[k], around[k])

    def share(k, p):
        return remote(part.at[p], cols.at[p, aligned(e, 4 * slim)], c_send.at[p, k], c_recv.at[p, k], (e ^ hops[k], s))

    def share_tags(k):
        return remote(tag_sum, all_tags.at[k], n_send.at[k], n_recv.at[k], (e ^ hops[k], s))

    def relay(k, p):
        view = cols.at[p, aligned(e ^ hops[k], 4 * slim)]
        return remote(view, view, c_send.at[p, 3 + k], c_recv.at[p, 3 + k], (e ^ 1, s))

    def relay_tags(k):
        return remote(all_tags.at[k], all_tags.at[3 + k], n_send.at[3 + k], n_recv.at[3 + k], (e ^ 1, s))

    def early_out(k):
        return remote(wo, wo_full.at[e, s], h_send.at[k], h_recv.at[k], around[k])

    def along_out(k):
        view = wo_full.at[e]
        return remote(view, view, h_send.at[3 + k], h_recv.at[3 + k], (e ^ hops[k], s))

    def relay_along(k):
        view = wo_full.at[e ^ hops[k]]
        return remote(view, view, h_send.at[6 + k], h_recv.at[6 + k], (e ^ 1, s))

    def give(r):
        return remote(att.at[pl.ds(r * rows, rows)], landed.at[s], a_send.at[r], a_recv.at[s ^ r], (e, r))

    cap = xs.shape[0] // 8

    def g_entry(place):
        return remote(gs.at[pl.ds(pl.multiple_of((e ^ ORDER[place]) * cap, 16), cap)], g_early.at[0, place],
                      e_send.at[place], e_recv.at[place], (e ^ ORDER[place], s))

    def g_hop(which, pair):
        places = pl.ds(2 * pair, 2) if which < 2 else pl.ds(2 * pair + which - 2, 1)
        return remote(g_early.at[(0, 0, 1, 2)[which], places], g_early.at[(1, 2, 3, 3)[which], places],
                      j_send.at[which, pair], j_recv.at[which, pair], (near_x, near_y, near_y, near_x)[which])

    def g_corner(pair):
        for which in range(2):
            g_hop(which, pair).wait_recv()
            g_hop(2 + which, pair).start()

    far = []

    def keep(src, dst):
        copy = pltpu.make_async_copy(src, dst, far_sem.at[len(far)])
        copy.start()
        far.append(copy)

    for k in range(3):
        for m in range(3):
            send_cols(k, m).start()
        send_tags(k).start()
    for k in range(2):
        send_tokens(k).start()
    for k in range(3):
        early_out(k).start()
    for m in range(3):
        got[m, aligned(s, slim), :] = weights[m][:, aligned(s, shard)]
    all_tokens[aligned(s, rows), :] = tokens[...]
    wo_full[e, s] = wo[...]
    hot_row, hot, slot, _, target_row = slots_of(ids_row[...], cap)
    level = lax.broadcasted_iota(jnp.int32, (8 * cap, rows), 0)
    takes = jnp.where((level == target_row[0]) | (level == target_row[1]), 1.0, 0.0).astype(low)
    total = misc[...].astype(full)
    for k in range(3):
        send_tags(k).wait_recv()
        total += tags[k].astype(full)
    tag_sum[...] = total.astype(low)
    for k in range(4):
        share_tags(k).start()
    for k in range(3):
        for m in range(3):
            send_cols(k, m).wait_recv()
    for p in range(2):
        for m in range(3):
            part[p, :, m * 128:(m + 1) * 128] = got[m, :, p * 128:(p + 1) * 128]
    for k in (3, 2, 1, 0):
        share(k, 0).start()
    for p in range(2):
        cols[p, aligned(e, 4 * slim), :] = part[p]
    gs[...] = contract(takes, cotangent[...], ((1,), (0,))).astype(low)
    for place in range(1, 4):
        g_entry(place).start()
    g_early[0, 0] = gs[pl.ds(pl.multiple_of(e * cap, 16), cap), :]
    keep(gs, gs_far)
    found = segment_scalars(lengths, parents, before_mem, reach_mem)
    stats[...] = jnp.zeros_like(stats)
    for r in range(4):
        index[r, :, :(r + 1) * rows] = pair_index(found, r * rows, rows, (r + 1) * rows)[0]
    for k in range(1, 4):
        share_tags(k).wait_recv()
        relay_tags(k).start()
    for k in range(2):
        send_tokens(k).wait_recv()
        pass_tokens(k).start()
    g_entry(1).wait_recv()
    for which in range(2):
        g_hop(which, 0).start()
    for k in range(1, 4):
        share(k, 0).wait_recv()
        relay(k, 0).start()
    for k in (3, 2, 1, 0):
        share(k, 1).start()
    for k in range(3):
        early_out(k).wait_recv()
    for k in (3, 2, 1, 0):
        along_out(k).start()
    share_tags(0).wait_recv()
    for k in range(1, 4):
        relay_tags(k).wait_recv()
    for k in range(7):
        total += all_tags[k].astype(full)
    params[...] = total
    gain = total[0:1]
    table[...] = bias_tables(params, s)

    def norm_block(q, carry):
        spot = aligned(s ^ q, rows)
        values = all_tokens[spot, :].astype(full)
        normed[spot, :] = (values * norm_factor(values) * gain).astype(low)
        return carry

    lax.fori_loop(0, 3, norm_block, 0)
    for k in range(2):
        pass_tokens(k).wait_recv()
    lax.fori_loop(3, 4, norm_block, 0)
    keep(all_tokens, all_tokens_far)

    def pair(p, carry):
        for which in range(2):
            @pl.when(p == which)
            def _():
                share(0, which).wait_recv()
                for k in range(1, 4):
                    relay(k, which).wait_recv()

        for r in range(4):
            out = contract(normed[r * rows:(r + 1) * rows, :], cols[p], ((1,), (0,)))
            first_part = out[:, 0:128].astype(low).astype(full) * HDIM ** (-0.5)
            qkv[p, r * rows:(r + 1) * rows, :] = jnp.concatenate([first_part, out[:, 128:]], axis=1).astype(low)

        for r in (3, 2, 1, 0):
            first, count = r * rows, (r + 1) * rows
            q = qkv[p, first:count, 0:128]
            k = qkv[p, 0:count, 128:256]
            v = qkv[p, 0:count, 256:384]
            lane = lax.broadcasted_iota(jnp.int32, (rows, 128), 1)
            results = []
            noted = stats[first:count, :]
            for side in range(2):
                mine = (lane // HDIM) == side
                scores = contract(jnp.where(mine, q, jnp.zeros_like(q)), k, ((1,), (1,)))
                scores = scores + looked_up(table[pl.ds(2 * p + side, 1), :], index[r, :, :count])
                peak = jnp.max(scores, axis=1, keepdims=True)
                expo = jnp.exp(scores - peak)
                mass = jnp.sum(expo, axis=1, keepdims=True)
                results.append(contract(expo.astype(low), v, ((1,), (0,))) * (1.0 / mass))
                noted = jnp.where(lane == 2 * p + side, peak + jnp.log(mass), noted)
            stats[first:count, :] = noted
            att[first:count, aligned(p, 128)] = jnp.where((lane // HDIM) == 0, results[0], results[1]).astype(low)

            @pl.when((p == 1) & (s != r))
            def _():
                give(r).start()

            if r == 3:
                @pl.when(p == 0)
                def _():
                    g_corner(0)
                    for i in (2, 3):
                        g_entry(i).wait_recv()
                    for which in range(2):
                        g_hop(which, 1).start()

                @pl.when(p == 1)
                def _():
                    g_corner(1)
            if r == 1:
                @pl.when(p == 1)
                def _():
                    for i in range(1, 4):
                        along_out(i).wait_recv()
                        relay_along(i).start()
            if r == 1:
                @pl.when(p == 0)
                def _():
                    for i in range(1, 4):
                        share(i, 1).wait_recv()
                        relay(i, 1).start()
        return carry

    lax.fori_loop(0, 2, pair, 0)
    keep(qkv, qkv_far)
    keep(cols, cols_far)
    keep(stats, stats_far)
    along_out(0).wait_recv()
    for k in range(1, 4):
        relay_along(k).wait_recv()
    keep(wo_full, wo_far)
    landed[s] = att[aligned(s, rows), :]
    total = tokens[...].astype(full)

    def out_rows(index):
        return wo_full[pl.ds(2 * index, 2)].reshape(shard, width)

    total += contract(landed[s], out_rows(s), ((1,), (0,)))
    for k in range(1, 4):
        remote(landed.at[s], landed.at[s ^ k], a_send.at[0], a_recv.at[k], (e, s ^ k)).wait_recv()
        total += contract(landed[s ^ k], out_rows(s ^ k), ((1,), (0,)))
    residual[...] = total
    keep(landed, att_far)
    _, _, normed, _, _, _, given = router_of(total, params[...], hot)
    xs[...] = contract(takes, normed, ((1,), (0,))).astype(low)
    at_slot = lax.broadcasted_iota(jnp.int32, (rows, 128), 1)
    by_slot = jnp.zeros((8, 128), full)
    for k in range(2):
        placed = jnp.where((at_slot == slot[k]) & (slot[k] < cap), given[k], 0.0)
        by_slot += lax.dot_general(hot_row[k], placed, (((1,), (0,)), ((), ())),
                                   precision=lax.Precision.HIGHEST, preferred_element_type=full)
    shares[...] = jnp.zeros_like(shares)
    for k in range(8):
        shares[k, 0:1, :] = by_slot[k:k + 1]
    for pair in range(2):
        for which in range(2):
            g_hop(2 + which, pair).wait_recv()
    keep(g_early, g_far)

    for place in range(1, 4):
        g_entry(place).wait_send()
    for pair in range(2):
        for which in range(4):
            g_hop(which, pair).wait_send()
    for k in range(2):
        send_tokens(k).wait_send()
        pass_tokens(k).wait_send()
    for k in range(3):
        for m in range(3):
            send_cols(k, m).wait_send()
        send_tags(k).wait_send()
        early_out(k).wait_send()
    for k in range(4):
        share_tags(k).wait_send()
        along_out(k).wait_send()
        for p in range(2):
            share(k, p).wait_send()
    for k in range(1, 4):
        relay_tags(k).wait_send()
        relay_along(k).wait_send()
        for p in range(2):
            relay(k, p).wait_send()
    for r in range(4):
        @pl.when(s != r)
        def _():
            give(r).wait_send()
    for copy in far:
        copy.wait()


def front(lengths, parents, tokens, cotangent, ids_row, wq, wk, wv, wo, gain_one, gain_two, bias, router_row):
    rows, width = tokens.shape
    slim, shard = wq.shape[0], width // 4
    cap = 10 * rows // 32
    low, full = jnp.bfloat16, jnp.float32
    vmem, smem, hbm = (pl.BlockSpec(memory_space=m) for m in (pltpu.VMEM, pltpu.SMEM, pl.ANY))
    dma = pltpu.SemaphoreType.DMA
    kept = (
        jax.ShapeDtypeStruct((4 * rows, width), low),
        jax.ShapeDtypeStruct((2, 4 * rows, 3 * shard // 2), low),
        jax.ShapeDtypeStruct((2, width, 3 * shard // 2), low),
        jax.ShapeDtypeStruct((16, width), full),
        jax.ShapeDtypeStruct((4, rows, shard), low),
        jax.ShapeDtypeStruct((4 * rows, 128), full),
        jax.ShapeDtypeStruct((8, 4, slim, width), low),
    )
    return pl.pallas_call(
        front_kernel,
        out_shape=(
            jax.ShapeDtypeStruct((8 * cap, width), low),
            jax.ShapeDtypeStruct((8 * cap, width), low),
            jax.ShapeDtypeStruct((8, 8, 128), full),
            jax.ShapeDtypeStruct((rows, width), full),
        ) + kept + (jax.ShapeDtypeStruct((4, 4, cap, width), low),),
        in_specs=[smem, smem] + [vmem] * 11,
        out_specs=(vmem, hbm, vmem, vmem, hbm, hbm, hbm, vmem, hbm, hbm, hbm, hbm),
        scratch_shapes=[
            pltpu.VMEM(kept[0].shape, low), pltpu.VMEM(kept[1].shape, low), pltpu.VMEM(kept[2].shape, low),
            pltpu.VMEM(kept[6].shape, low), pltpu.VMEM((4 * rows, shard), low), pltpu.VMEM(kept[5].shape, full),
            pltpu.VMEM((3, 4 * slim, shard), low), pltpu.VMEM((2, 4 * slim, 3 * shard // 2), low),
            pltpu.VMEM((4 * rows, width), low),
            pltpu.VMEM((16, width), low), pltpu.VMEM((3, 16, width), low), pltpu.VMEM((16, width), low),
            pltpu.VMEM((7, 16, width), low),
            pltpu.VMEM((4, rows, 4 * rows), jnp.int32), pltpu.VMEM((8, 128), full),
            pltpu.VMEM((4, rows, shard), low),
            pltpu.VMEM((8 * cap, width), low), pltpu.VMEM((4, 4, cap, width), low),
            pltpu.SMEM((16,), jnp.int32), pltpu.SMEM((16,), jnp.int32),
            dma((4,)), dma((4,)), dma((3, 3)), dma((3, 3)), dma((3,)), dma((3,)),
            dma((2, 7)), dma((2, 7)), dma((7,)), dma((7,)),
            dma((10,)), dma((10,)), dma((4,)), dma((4,)),
            dma((4,)), dma((4,)), dma((4, 2)), dma((4, 2)), dma((8,)),
        ],
        compiler_params=pltpu.CompilerParams(
            collective_id=2, has_side_effects=True, vmem_limit_bytes=VMEM_LIMIT
        ),
        cost_estimate=pl.CostEstimate(flops=40 * rows * width * shard, bytes_accessed=24 << 20, transcendentals=8 * rows * rows * 16),
        name="front",
    )(lengths, parents, tokens, cotangent, ids_row, wq, wk, wv, wo, gain_one, gain_two, bias, router_row)


def pair_index_across(found, first, rows, count):
    ids = first + lax.broadcasted_iota(jnp.int32, (1, rows), 1)
    keys = lax.broadcasted_iota(jnp.int32, (count, 1), 0)
    place, reach, _ = token_columns(found, ids)
    key_place, _, key_own = token_columns(found, keys)
    seen = ((reach & key_own) != 0) & (keys <= ids)
    return jnp.where(seen, jnp.minimum(place - key_place, LAST - 1), LAST)


def near_keys(found, first, rows):
    ids = first + lax.broadcasted_iota(jnp.int32, (rows, 1), 0)
    place, reach, _ = token_columns(found, ids)
    step = lax.broadcasted_iota(jnp.int32, (rows, LAST + 1), 1)
    wanted = place - step
    spot = jnp.full((rows, LAST + 1), -1, jnp.int32)
    for k, (start, before, _, length) in enumerate(found):
        inside = ((reach & (1 << k)) != 0) & (wanted >= before) & (wanted < before + length)
        spot = jnp.where(inside, wanted + (start - before), spot)
    return jnp.where(step == LAST, -1, spot)


GROUPS = ((0, 3), (3, 3))


def back_kernel(
    lengths, parents, ids_row, params, ret_s, po_far, ret_b_far, residual_far, cotangent_far,
    wo_far, qkv_far, cols_far, all_tokens_far, att_far, stats_far,
    layer_out_far, tokens_grad, dwq, dwk, dwv, dwo, small_sum,
    po0, po2, ro, ro2, ret_o, ret_b, residual, cotangent, layer_out, wo, qkv, cols, all_tokens, att, stats, datt, datt_own, aog_own, residual_grad,
    o_halves, o_core, o_sums, o_z, o_final, o_seq, index, spots, lse, table, near, dk, dv, dqkv, normed,
    halves, core_got, sums, z_got, final, final_got, parts, first_got, second_got, mine, tally, tally_got, square, square_got,
    before_mem, reach_mem,
    load_sem, d_send, d_recv, w_send, w_recv, core_send, core_recv, z_send, z_recv, a_send, a_recv,
    n_send, n_recv, m_send, m_recv, o_send, o_recv, r_send, r_recv, q_send, q_recv, own_sem,
):
    e, s = lax.axis_index(EXPERT), lax.axis_index(SEQ)
    z, c = e // 2, lax.rem(e, 2)
    near_x, near_y = (e, s ^ 1), (e, s ^ 2)
    around = [(e, s ^ k) for k in range(1, 4)]
    hops = (1,) + ZHOPS
    full, low = jnp.float32, jnp.bfloat16
    high = lax.Precision.HIGHEST
    rows, width = residual.shape
    shard = att.shape[2]
    slim = dwq.shape[0]
    cap = ret_b.shape[0] // 8
    half = shard // 2
    pairs = (
        (residual_far, residual), (cotangent_far, cotangent), (ret_b_far, ret_b), (wo_far, wo), (po_far.at[0], po0),
        (att_far, att), (stats_far, stats), (qkv_far, qkv), (all_tokens_far, all_tokens), (cols_far, cols),
        (po_far.at[2, 0], po2.at[0]), (po_far.at[1, 1], po2.at[1]),
    )
    loads = [pltpu.make_async_copy(src, dst, load_sem.at[k]) for k, (src, dst) in enumerate(pairs)]
    for load in loads:
        load.start()
    greet(around + [(e ^ d, s) for d in range(1, 8)])

    def o_copy(side, which, zone):
        first, second = ((near_x, near_y), (near_y, near_x))[side]
        two = pl.ds(2 * zone, 2)
        if which == 2:
            src, dst = po2.at[side, two], ro2.at[side, two]
        else:
            src, dst = po_far.at[(1 + side, 3)[which], side, two], ro.at[which, side, two]
        return remote(src, dst, o_send.at[side, which, zone], o_recv.at[side, which, zone], second if which == 2 else first)

    def block(index):
        return pl.ds(pl.multiple_of(index * cap, 16), cap)

    def return_rows(place):
        return remote(po0.at[place % 2, place // 2], ret_o.at[block(e)], r_send.at[place], r_recv.at[place],
                      (e ^ ORDER[place], s))

    def start_outs(zone):
        for which in (1, 0):
            for side in range(2):
                o_copy(side, which, zone).start()

    def add_outs(zone):
        for side in range(2):
            o_copy(side, 1, zone).wait_recv()
            for i in (2 * zone, 2 * zone + 1):
                po2[side, i] = (po2[side, i].astype(full) + ro[1, side, i].astype(full)).astype(low)
            o_copy(side, 2, zone).start()

    def finish_outs(zone):
        for side in range(2):
            o_copy(side, 0, zone).wait_recv()
            o_copy(side, 2, zone).wait_recv()
            for i in (2 * zone, 2 * zone + 1):
                po0[side, i] = (
                    po0[side, i].astype(full) + ro[0, side, i].astype(full) + ro2[side, i].astype(full)
                ).astype(low)
                if 2 * i + side:
                    return_rows(2 * i + side).start()
                else:
                    ret_o[block(e), :] = po0[0, 0]

    start_outs(1)
    loads[0].wait()

    held = residual[...]
    _, hot, slot, target, _ = slots_of(ids_row[...], cap)
    scale, unit, unrouted, router, prob, chosen_sum, shares = router_of(held, params[...], hot)
    place = lax.broadcasted_iota(jnp.int32, (rows, 8 * cap), 1)
    takes = jnp.where((place == target[0]) | (place == target[1]), 1.0, 0.0).astype(low)
    at_slot = lax.broadcasted_iota(jnp.int32, (rows, 128), 1)
    dots = jnp.concatenate([ret_s[k, 0:1, :] for k in range(8)], axis=0)
    share_grad = []
    for k in range(2):
        mine_dots = lax.dot_general(hot[k], dots, (((1,), (0,)), ((), ())), precision=high, preferred_element_type=full)
        share_grad.append(jnp.sum(
            jnp.where((at_slot == slot[k]) & (slot[k] < cap), mine_dots, 0.0), axis=1, keepdims=True))
    for load in loads[1:4]:
        load.wait()
    grad = cotangent[...].astype(full)
    inner = shares[0] * share_grad[0] + shares[1] * share_grad[1]
    prob_grad = sum(hot[k] * ((share_grad[k] - inner) / chosen_sum) for k in range(2))
    logit_grad = prob * (prob_grad - jnp.sum(prob * prob_grad, axis=1, keepdims=True))
    normed_grad = contract(takes, ret_b[...], ((1,), (0,))) + lax.dot_general(
        logit_grad, router, (((1,), (0,)), ((), ())), precision=high, preferred_element_type=full
    )
    unit_grad = normed_grad * params[1:2]
    passed = grad + scale * (unit_grad - unit * jnp.mean(unit_grad * unit, axis=1, keepdims=True))
    residual_grad[...] = passed
    aog_own[...] = passed.astype(low)
    datt_own[...] = contract(aog_own[...], wo[...], ((1,), (1,))).astype(low)

    def give(k):
        return remote(datt_own.at[:, aligned(s ^ (k + 1), shard)], datt.at[aligned(s, rows)],
                      d_send.at[k], d_recv.at[k], around[k])

    for k in (2, 0, 1):
        give(k).start()

    def wide_core():
        return remote(o_halves.at[1 - c], o_core, w_send.at[0], w_recv.at[0], (e ^ 1, s))

    def wide_z(k):
        return remote(o_sums.at[z ^ k], o_z.at[k - 1], w_send.at[k], w_recv.at[k], (e ^ (2 * k), s))

    def wide_seq(k):
        return remote(o_final.at[aligned(s ^ (k + 1), slim)], o_seq.at[k], w_send.at[4 + k], w_recv.at[4 + k], around[k])

    for load in loads[4:]:
        load.wait()

    def output_zone(j, carry):
        part = contract(att[j], aog_own[...], ((0,), (0,)))
        for i in range(2):
            o_halves[i, j] = part[i * half:(i + 1) * half].astype(low)
        return carry

    lax.fori_loop(0, 4, output_zone, 0)
    wide_core().start()
    datt[aligned(s, rows), :] = datt_own[:, aligned(s, shard)]
    tally[0] = jnp.zeros((16, width), full)
    tally[0, 1:2] = jnp.sum(normed_grad * unit, axis=0, keepdims=True)
    lane = lax.broadcasted_iota(jnp.int32, (1, width), 1)
    tally[0, 3:4] = jnp.where(lane == 0, jnp.sum(held * held), 0.0)
    tally[0, 8:16] = lax.dot_general(logit_grad, unrouted.astype(full), (((0,), (0,)), ((), ())),
                                     precision=high, preferred_element_type=full)
    wide_core().wait_recv()
    for j in range(4):
        o_sums[j] = (o_halves[c, j].astype(full) + o_core[j].astype(full)).astype(low)
    for k in range(1, 4):
        wide_z(k).start()
    found = segment_scalars(lengths, parents, before_mem, reach_mem)
    table[...] = bias_tables(params, s)
    near[...] = jnp.zeros_like(near)
    for r in range(4):
        index[r, :(r + 1) * rows] = pair_index_across(found, r * rows, rows, (r + 1) * rows)
        spots[r] = near_keys(found, r * rows, rows)
        turned = jnp.transpose(stats[r * rows:(r + 1) * rows, :])
        for h in range(4):
            lse[h, r] = turned[h:h + 1]
    gain = params[0:1]

    def units(q):
        values = all_tokens[aligned(s ^ q, rows), :].astype(full)
        factor = norm_factor(values)
        return values * factor, factor

    def norm_block(q, carry):
        normed[aligned(s ^ q, rows), :] = (units(q)[0] * gain).astype(low)
        return carry

    lax.fori_loop(0, 4, norm_block, 0)

    def core_copy(g):
        slots = pl.ds(*GROUPS[g])
        return remote(halves.at[1 - c, slots], core_got.at[slots], core_send.at[g], core_recv.at[g], (e ^ 1, s))

    def z_copy(g, k):
        slots = pl.ds(*GROUPS[g])
        return remote(sums.at[slots, z ^ k], z_got.at[k - 1, slots], z_send.at[g, k - 1], z_recv.at[g, k - 1],
                      (e ^ (2 * k), s))

    def a_copy(g, k):
        slots = pl.ds(*GROUPS[g])
        return remote(final.at[slots, aligned(s ^ (k + 1), slim)], final_got.at[s, slots],
                      a_send.at[g, k], a_recv.at[g, k], around[k])

    def add_core(g):
        core_copy(g).wait_recv()
        first, amount = GROUPS[g]
        for slot in range(first, first + amount):
            for j in range(4):
                sums[slot, j] = (halves[c, slot, j].astype(full) + core_got[slot, j].astype(full)).astype(low)
        for k in range(1, 4):
            z_copy(g, k).start()

    def finish_grad(g):
        first, amount = GROUPS[g]
        for k in range(1, 4):
            z_copy(g, k).wait_recv()
        for slot in range(first, first + amount):
            block = sums[slot, z].astype(full)
            for k in range(1, 4):
                block += z_got[k - 1, slot].astype(full)
            final[slot] = block
        for k in range(3):
            a_copy(g, k).start()
        for slot in range(first, first + amount):
            final_got[s, slot] = final[slot, aligned(s, slim)]

    for k in range(3):
        give(k).wait_recv()
    add_outs(1)

    def pair(p, carry):
        lanes = aligned(p, 128)
        dk[...] = jnp.zeros_like(dk)
        dv[...] = jnp.zeros_like(dv)
        for r in (3, 2, 1, 0):
            first, count = r * rows, (r + 1) * rows
            q = qkv[p, first:count, 0:128]
            k = qkv[p, 0:count, 128:256]
            v = qkv[p, 0:count, 256:384]
            g = datt[first:count, lanes]
            lane = lax.broadcasted_iota(jnp.int32, (rows, 128), 1)
            lane_long = lax.broadcasted_iota(jnp.int32, (count, 128), 1)
            spot = spots[r]
            spot_lane, spot_block = spot & 127, jnp.where(spot < 0, -1, spot >> 7)
            dq = []
            key_sum, value_sum = 0.0, 0.0
            for side in range(2):
                mine_lanes = (lane // HDIM) == side
                q_side = jnp.where(mine_lanes, q, jnp.zeros_like(q))
                g_side = jnp.where(mine_lanes, g, jnp.zeros_like(g))
                scores = contract(k, q_side, ((1,), (1,)))
                scores = scores + looked_up(table[pl.ds(2 * p + side, 1), :], index[r, :count])
                soft = jnp.exp(scores - lse[2 * p + side, r])
                dprob = contract(v, g_side, ((1,), (1,)))
                delta = jnp.sum(soft * dprob, axis=0, keepdims=True)
                turned = soft * (dprob - delta)
                score_grad = turned.astype(low)
                key_sum = key_sum + contract(score_grad, q_side, ((1,), (0,)))
                value_sum = value_sum + contract(soft.astype(low), g_side, ((1,), (0,)))
                wide = jnp.transpose(turned)
                with_ones = jnp.where((lane_long // HDIM) == side, k, jnp.ones_like(k))
                part = contract(wide.astype(low), with_ones, ((1,), (0,)))
                dq.append(part)
                close = jnp.zeros((rows, 128), full)
                for b in range(count // 128):
                    taken = jnp.take_along_axis(wide[:, b * 128:(b + 1) * 128], spot_lane, axis=1)
                    close = jnp.where(spot_block == b, taken, close)
                near[0, 2 * p + side] += jnp.sum(close.reshape(rows // 8, 8, 128), axis=0)
                rest = jnp.where(mine_lanes, 0.0, part)
                near[1, 2 * p + side] += jnp.sum(rest.reshape(rows // 8, 8, 128), axis=0)
            dqkv[p, first:count, 0:128] = (jnp.where((lane // HDIM) == 0, dq[0], dq[1]) * HDIM ** (-0.5)).astype(low)
            dk[0:count] += key_sum
            dv[0:count] += value_sum

            if r == 3:
                @pl.when(p == 0)
                def _():
                    finish_outs(1)
                    start_outs(0)

                @pl.when(p == 1)
                def _():
                    add_core(0)
            if r == 1:
                @pl.when(p == 1)
                def _():
                    add_outs(0)
        dqkv[p, :, 128:256] = dk[...].astype(low)
        dqkv[p, :, 256:384] = dv[...].astype(low)

        def qkv_zone(j, carry):
            block = contract(normed[:, aligned(j, shard)], dqkv[p], ((0,), (0,)))
            for m in range(3):
                for i in range(2):
                    halves[i, 3 * p + m, j] = block[i * half:(i + 1) * half, m * 128:(m + 1) * 128].astype(low)
            return carry

        lax.fori_loop(0, 4, qkv_zone, 0)

        @pl.when(p == 0)
        def _():
            core_copy(0).start()

        @pl.when(p == 1)
        def _():
            core_copy(1).start()
        return carry

    lax.fori_loop(0, 2, pair, 0)

    def n_copy(kind, which):
        one, two = ((near_x, near_y), (near_y, near_x))[kind]
        if which < 2:
            src = parts.at[(1 + kind, 3)[which], kind]
            return remote(src, first_got.at[kind, which], n_send.at[kind, which], n_recv.at[kind, which], one)
        return remote(parts.at[2 - kind, kind], second_got.at[kind], n_send.at[kind, 2], n_recv.at[kind, 2], two)

    def back_block(i, carry):
        q = 3 - i
        total = jnp.zeros((rows, width), full)
        for p in range(2):
            total += contract(dqkv[p, aligned(s ^ q, rows), :], cols[p], ((1,), (1,)))
        tally[0, 0:1] += jnp.sum(total * units(q)[0], axis=0, keepdims=True)
        mine[...] = total
        for kind in range(2):
            parts[q, kind] = total[:, kind * (width // 2):(kind + 1) * (width // 2)].astype(low)

        @pl.when(i == 0)
        def _():
            n_copy(0, 1).start()
            n_copy(1, 1).start()
            add_core(1)

        @pl.when(i == 1)
        def _():
            n_copy(1, 0).start()

        @pl.when(i == 2)
        def _():
            n_copy(0, 0).start()
        return carry

    lax.fori_loop(0, 4, back_block, 0)
    finish_outs(0)
    for k in range(1, 4):
        wide_z(k).wait_recv()
    whole = o_sums[z].astype(full)
    for k in range(3):
        whole += o_z[k].astype(full)
    o_final[...] = whole.astype(low)
    for k in range(3):
        wide_seq(k).start()

    close, rest = (
        jnp.concatenate([jnp.sum(near[kind, h], axis=0, keepdims=True) for h in range(8)], axis=0) for kind in range(2)
    )
    far = jnp.sum(rest, axis=1, keepdims=True) / HDIM - jnp.sum(close, axis=1, keepdims=True)
    spot = lax.broadcasted_iota(jnp.int32, close.shape, 1)
    by_distance = jnp.where(spot == LAST, far, close)
    lane = lax.broadcasted_iota(jnp.int32, (128, BUCKETS * HEADS), 1)
    distance = lax.broadcasted_iota(jnp.int32, (128, BUCKETS * HEADS), 0)
    hot_bucket = jnp.where((lane // HEADS) == bucket_of(distance), 1.0, 0.0)
    spread = lax.dot_general(by_distance, hot_bucket, (((1,), (0,)), ((), ())), precision=high, preferred_element_type=full)
    head = lax.broadcasted_iota(jnp.int32, spread.shape, 0)
    lane = lax.broadcasted_iota(jnp.int32, spread.shape, 1)
    here = ((lane % HEADS) == s * (HEADS // 4) + head) & (head < HEADS // 4)
    tally[0, 2:3, 0:BUCKETS * HEADS] = jnp.sum(jnp.where(here, spread, 0.0), axis=0, keepdims=True)

    def m_copy(stage, k):
        slot = (0, 3, 4)[stage] + k
        peer = (around[k], (e ^ 1, s), (e ^ (2 * (k + 1)), s))[stage]
        return remote(tally.at[stage], tally_got.at[slot], m_send.at[slot], m_recv.at[slot], peer)

    for k in range(3):
        m_copy(0, k).start()
    for kind in range(2):
        n_copy(kind, 1).wait_recv()
        group = 2 - kind
        parts[group, kind] = (parts[group, kind].astype(full) + first_got[kind, 1].astype(full)).astype(low)
        n_copy(kind, 2).start()
    finish_grad(0)
    total = tally[0]
    for k in range(3):
        m_copy(0, k).wait_recv()
        total += tally_got[k]
    tally[1] = total
    m_copy(1, 0).start()

    for place in range(1, 8):
        return_rows(place).wait_recv()
    mixture = contract(takes, ret_o[...], ((1,), (0,)))
    layer_out[...] = (residual[...] + mixture).astype(low)
    layer_done = pltpu.make_async_copy(layer_out, layer_out_far, own_sem)
    layer_done.start()
    squares = jnp.full((8, 128), jnp.sum(mixture * mixture), full)

    def q_copy(stage, k):
        slot = (0, 3, 4)[stage] + k
        peer = (around[k], (e ^ 1, s), (e ^ (2 * (k + 1)), s))[stage]
        return remote(square.at[stage], square_got.at[slot], q_send.at[slot], q_recv.at[slot], peer)

    square[0] = squares
    for k in range(3):
        q_copy(0, k).start()
    finish_grad(1)
    m_copy(1, 0).wait_recv()
    total = total + tally_got[3]
    tally[2] = total
    for k in range(3):
        m_copy(2, k).start()
    for k in range(3):
        q_copy(0, k).wait_recv()
        squares += square_got[k]
    square[1] = squares
    q_copy(1, 0).start()
    for kind in range(2):
        n_copy(kind, 0).wait_recv()
        n_copy(kind, 2).wait_recv()
        lanes = slice(kind * (width // 2), (kind + 1) * (width // 2))
        mine[:, lanes] += first_got[kind, 0].astype(full) + second_got[kind].astype(full)
    unit, scale = units(0)
    unit_grad = mine[...] * gain
    tokens_grad[...] = residual_grad[...] + scale * (
        unit_grad - unit * jnp.mean(unit_grad * unit, axis=1, keepdims=True)
    )
    q_copy(1, 0).wait_recv()
    squares += square_got[3]
    square[2] = squares
    for k in range(3):
        q_copy(2, k).start()
    for g in range(2):
        for k in range(3):
            a_copy(g, k).wait_recv()
    for m, out in enumerate((dwq, dwk, dwv)):
        for i in range(2):
            for j in range(4):
                out[:, j * shard + i * 128:j * shard + (i + 1) * 128] = final_got[j, m + 3 * i]
    whole = o_final[aligned(s, slim), :].astype(full)
    for k in range(3):
        wide_seq(k).wait_recv()
        whole += o_seq[k].astype(full)
    dwo[...] = whole
    for k in range(3):
        m_copy(2, k).wait_recv()
        total += tally_got[4 + k]
    for k in range(3):
        q_copy(2, k).wait_recv()
        squares += square_got[4 + k]
    lane = lax.broadcasted_iota(jnp.int32, (1, 128), 1)
    small_sum[...] = total
    small_sum[3:4, 0:128] = jnp.where(lane == 1, squares[0:1], total[3:4, 0:128])
    layer_done.wait()
    wide_core().wait_send()
    for k in range(3):
        give(k).wait_send()
        wide_z(k + 1).wait_send()
        wide_seq(k).wait_send()
        for g in range(2):
            z_copy(g, k + 1).wait_send()
            a_copy(g, k).wait_send()
    for g in range(2):
        core_copy(g).wait_send()
    for kind in range(2):
        for which in range(3):
            n_copy(kind, which).wait_send()
    for stage, amount in ((0, 3), (1, 1), (2, 3)):
        for k in range(amount):
            m_copy(stage, k).wait_send()
            q_copy(stage, k).wait_send()
    for place in range(1, 8):
        return_rows(place).wait_send()
    for side in range(2):
        for which in range(3):
            for zone in range(2):
                o_copy(side, which, zone).wait_send()


def back(lengths, parents, ids_row, params, ret_s, part_o, ret_b, residual, cotangent, wo, qkv, cols, all_tokens, att, stats):
    rows, width = residual.shape
    shard = att.shape[2]
    slim = width // 32
    low, full = jnp.bfloat16, jnp.float32
    vmem, smem, hbm = (pl.BlockSpec(memory_space=m) for m in (pltpu.VMEM, pltpu.SMEM, pl.ANY))
    dma = pltpu.SemaphoreType.DMA
    half = shard // 2
    return pl.pallas_call(
        back_kernel,
        out_shape=(
            jax.ShapeDtypeStruct((rows, width), low),
            jax.ShapeDtypeStruct((rows, width), full),
        ) + (jax.ShapeDtypeStruct((slim, width), full),) * 4 + (jax.ShapeDtypeStruct((16, width), full),),
        in_specs=[smem, smem] + [vmem] * 3 + [hbm] * 10,
        out_specs=(hbm,) + (vmem,) * 6,
        scratch_shapes=[
            pltpu.VMEM(part_o.shape[1:], low), pltpu.VMEM(part_o.shape[1:], low), pltpu.VMEM((2,) + part_o.shape[1:], low),
            pltpu.VMEM(part_o.shape[1:], low),
            pltpu.VMEM(ret_b.shape, low), pltpu.VMEM(ret_b.shape, low), pltpu.VMEM((rows, width), full),
            pltpu.VMEM((rows, width), low), pltpu.VMEM((rows, width), low),
            pltpu.VMEM((width, width), low), pltpu.VMEM(qkv.shape, low), pltpu.VMEM(cols.shape, low),
            pltpu.VMEM(all_tokens.shape, low), pltpu.VMEM(att.shape, low), pltpu.VMEM(stats.shape, full),
            pltpu.VMEM((4 * rows, shard), low), pltpu.VMEM((rows, width), low),
            pltpu.VMEM((rows, width), low), pltpu.VMEM((rows, width), full),
            pltpu.VMEM((2, 4, half, width), low), pltpu.VMEM((4, half, width), low),
            pltpu.VMEM((4, half, width), low), pltpu.VMEM((3, half, width), low),
            pltpu.VMEM((half, width), low), pltpu.VMEM((3, slim, width), low),
            pltpu.VMEM((4, 4 * rows, rows), jnp.int32), pltpu.VMEM((4, rows, 128), jnp.int32),
            pltpu.VMEM((4, 4, 1, rows), full), pltpu.VMEM((8, 128), full), pltpu.VMEM((2, 8, 8, 128), full),
            pltpu.VMEM((4 * rows, 128), full), pltpu.VMEM((4 * rows, 128), full),
            pltpu.VMEM((2, 4 * rows, 3 * shard // 2), low), pltpu.VMEM((4 * rows, width), low),
            pltpu.VMEM((2, 6, 4, half, half), low), pltpu.VMEM((6, 4, half, half), low),
            pltpu.VMEM((6, 4, half, half), low), pltpu.VMEM((3, 6, half, half), low),
            pltpu.VMEM((6, half, half), full), pltpu.VMEM((4, 6, slim, half), full),
            pltpu.VMEM((4, 2, rows, width // 2), low), pltpu.VMEM((2, 2, rows, width // 2), low),
            pltpu.VMEM((2, rows, width // 2), low), pltpu.VMEM((rows, width), full),
            pltpu.VMEM((3, 16, width), full), pltpu.VMEM((7, 16, width), full),
            pltpu.VMEM((3, 8, 128), full), pltpu.VMEM((7, 8, 128), full),
            pltpu.SMEM((16,), jnp.int32), pltpu.SMEM((16,), jnp.int32),
            dma((12,)), dma((3,)), dma((3,)), dma((7,)), dma((7,)), dma((2,)), dma((2,)),
            dma((2, 3)), dma((2, 3)), dma((2, 3)), dma((2, 3)), dma((2, 3)), dma((2, 3)), dma((7,)), dma((7,)),
            dma((2, 3, 2)), dma((2, 3, 2)), dma((8,)), dma((8,)), dma((7,)), dma((7,)), dma,
        ],
        compiler_params=pltpu.CompilerParams(
            collective_id=5, has_side_effects=True, vmem_limit_bytes=VMEM_LIMIT
        ),
        cost_estimate=pl.CostEstimate(flops=120 * rows * width * shard, bytes_accessed=20 << 20, transcendentals=8 * rows * rows * 16),
        name="back",
    )(lengths, parents, ids_row, params, ret_s, part_o, ret_b, residual, cotangent, wo, qkv, cols, all_tokens, att, stats)


def emit_kernel(*refs):
    large, small = refs[:9], refs[9]
    out, (gain_one, gain_two, bias, router, roots) = refs[10:19], refs[19:24]
    held, wide, in_sem, out_sem = refs[24:33], refs[33:36], refs[36], refs[37]
    comes, goes = [], []
    for k, (src, mid, dst) in enumerate(zip(large, held, out)):
        pieces = 4 if k >= 6 else 1
        amount = src.shape[0] // pieces
        for i in range(pieces):
            part = pl.ds(i * amount, amount)
            comes.append(pltpu.make_async_copy(src.at[part], mid.at[part], in_sem.at[len(comes)]))
            last = wide[k - 6] if k >= 6 else mid
            goes.append(pltpu.make_async_copy(last.at[part], dst.at[part], out_sem.at[len(goes)]))
    order = list(range(6, 18)) + list(range(6))
    for k in order:
        comes[k].start()
    place = lax.axis_index(EXPERT) * 4 + lax.axis_index(SEQ)
    width = small.shape[1]

    def own(length):
        lane = lax.broadcasted_iota(jnp.int32, (length, width), 1)
        down = lax.broadcasted_iota(jnp.int32, (length, width), 0)
        return jnp.where(lane == place * length + down, 1.0, 0.0)

    def picked(left, right):
        return lax.dot_general(left, right, (((1,), (1,)), ((), ())),
                               precision=lax.Precision.HIGHEST, preferred_element_type=jnp.float32)

    for k in order:
        comes[k].wait()
        if k >= 6:
            which, i = (k - 6) // 4, (k - 6) % 4
            amount = held[6].shape[0] // 4
            part = slice(i * amount, (i + 1) * amount)
            wide[which][part] = held[6 + which][part].astype(jnp.float32)
        goes[k].start()
    slim = gain_one.shape[1]
    ours = own(slim)
    gains = picked(small[0:8], ours)
    gain_one[...] = gains[0:1]
    gain_two[...] = gains[1:2]
    bias[...] = picked(small[0:8], own(bias.shape[1]))[2:3]
    router[...] = picked(small[8:16], ours)
    roots[...] = jnp.sqrt(small[3:4, 0:2] / (32 * large[0].shape[0] * width))
    for copy in goes:
        copy.wait()


def emit(large, small):
    full = jnp.float32
    width = small.shape[1]
    vmem, hbm = pl.BlockSpec(memory_space=pltpu.VMEM), pl.BlockSpec(memory_space=pl.ANY)
    slim = width // 32
    shapes = ((1, slim), (1, slim), (1, BUCKETS * HEADS // 32), (8, slim), (1, 2))
    return pl.pallas_call(
        emit_kernel,
        out_shape=tuple(jax.ShapeDtypeStruct(x.shape, x.dtype) for x in large[:6])
        + tuple(jax.ShapeDtypeStruct(x.shape, full) for x in large[6:])
        + tuple(jax.ShapeDtypeStruct(shape, full) for shape in shapes),
        in_specs=[hbm] * 9 + [vmem],
        out_specs=(hbm,) * 9 + (vmem,) * 5,
        scratch_shapes=[pltpu.VMEM(x.shape, x.dtype) for x in large]
        + [pltpu.VMEM(x.shape, full) for x in large[6:]]
        + [pltpu.SemaphoreType.DMA((18,)), pltpu.SemaphoreType.DMA((18,))],
        compiler_params=pltpu.CompilerParams(vmem_limit_bytes=VMEM_LIMIT),
        name="emit",
    )(*large, small)


def per_device_kernels(
    tokens, cotangent, expert_ids, segment_lengths, segment_parents, attention_gain,
    query_weight, key_weight, value_weight, output_weight, bias_table, feedforward_gain,
    router_weight, gate_weight, up_weight, down_weight,
):
    ids_row = expert_ids.T
    send_rows, grad_rows, shares, residual, all_tokens, qkv, cols, params, att, stats, wo, g_early = front(
        segment_lengths, segment_parents, tokens, cotangent, ids_row, query_weight, key_weight, value_weight,
        output_weight, attention_gain[None], feedforward_gain[None], bias_table[None], router_weight.T,
    )
    part_out, grad_back, dots, gate_term, up_term, down_term = experts(
        send_rows, grad_rows, shares, g_early, gate_weight[0], up_weight[0], down_weight[0]
    )
    layer_out, tokens_grad, dwq, dwk, dwv, dwo, totals = back(
        segment_lengths, segment_parents, ids_row, params, dots, part_out, grad_back, residual, cotangent,
        wo.reshape(D, D), qkv, cols, all_tokens, att, stats,
    )
    large = (layer_out, tokens_grad, dwq, dwk, dwv, dwo, gate_term, up_term, down_term)
    *large, gain_one, gain_two, bias, router, roots = emit(large, totals)
    layer_out, tokens_grad, dwq, dwk, dwv, dwo, gate_term, up_term, down_term = large
    return (
        layer_out, tokens_grad, gain_one[0], dwq, dwk, dwv, dwo, bias[0], gain_two[0], router.T,
        gate_term[None], up_term[None], down_term[None], roots[0],
    )


def per_device_general(
    tokens,
    cotangent,
    expert_ids,
    segment_lengths,
    segment_parents,
    attention_gain,
    query_weight,
    key_weight,
    value_weight,
    output_weight,
    bias_table,
    feedforward_gain,
    router_weight,
    gate_weight,
    up_weight,
    down_weight,
):
    seq_count = lax.axis_size(SEQ)
    seq_place = lax.axis_index(SEQ)
    all_count = lax.axis_size(EXPERT) * seq_count
    row_count = tokens.shape[0]
    experts = lax.axis_size(EXPERT) * gate_weight.shape[0]
    capacity = 10 * row_count // (4 * experts)
    score_scale = HDIM ** (-0.5)
    gathered = (
        lax.all_gather(attention_gain, BOTH, axis=0, tiled=True),
        lax.all_gather(query_weight, BOTH, axis=0, tiled=True),
        lax.all_gather(key_weight, BOTH, axis=0, tiled=True),
        lax.all_gather(value_weight, BOTH, axis=0, tiled=True),
        lax.all_gather(output_weight, BOTH, axis=0, tiled=True),
        lax.all_gather(bias_table, BOTH, axis=0, tiled=True),
        lax.all_gather(feedforward_gain, BOTH, axis=0, tiled=True),
        lax.all_gather(router_weight, BOTH, axis=0, tiled=True),
    )
    gain_one, query_full, key_full, value_full, output_full, bias_flat, gain_two, router_full = (
        gathered
    )
    bias_grid = bias_flat.reshape(BUCKETS, HEADS)
    starts, before, reaches = tree_tables(segment_lengths[0], segment_parents[0])
    own_rows = seq_place * row_count + jnp.arange(row_count, dtype=jnp.int32)
    own_meta = token_info(own_rows, starts, before, reaches)
    tokens_float = tokens.astype(jnp.float32)
    scale_one = norm_factor(tokens_float)
    unit_one = tokens_float * scale_one
    normed_one = (unit_one * gain_one.astype(jnp.float32)).astype(jnp.bfloat16)
    queries = (
        jnp.dot(normed_one, query_full, preferred_element_type=jnp.float32)
        .astype(jnp.bfloat16)
        .reshape(row_count, HEADS, HDIM)
    )
    keys_own = (
        jnp.dot(normed_one, key_full, preferred_element_type=jnp.float32)
        .astype(jnp.bfloat16)
        .reshape(row_count, HEADS, HDIM)
    )
    values_own = (
        jnp.dot(normed_one, value_full, preferred_element_type=jnp.float32)
        .astype(jnp.bfloat16)
        .reshape(row_count, HEADS, HDIM)
    )
    row_peak = jnp.full((HEADS, row_count), NEGATIVE, jnp.float32)
    key_piece = lax.all_gather(keys_own, SEQ, axis=0, tiled=True)
    value_piece = lax.all_gather(values_own, SEQ, axis=0, tiled=True)
    key_rows = jnp.arange(key_piece.shape[0], dtype=jnp.int32)
    visible, onehot, pair_bias = pair_terms(
        own_meta, token_info(key_rows, starts, before, reaches), own_rows, key_rows, bias_grid
    )
    scores = masked_scores(queries, key_piece, visible, pair_bias)
    new_peak = jnp.maximum(row_peak, jnp.max(scores, axis=-1))
    expo = jnp.exp(scores - new_peak[:, :, None])
    row_total = jnp.sum(expo, axis=-1)
    summed = jnp.einsum(
        SPEC_2, expo.astype(jnp.bfloat16), value_piece, preferred_element_type=jnp.float32
    )
    row_peak, row_total, summed = (new_peak, row_total, summed)
    log_total = row_peak + jnp.log(row_total)
    attended_float = summed / jnp.transpose(row_total)[:, :, None]
    attended = attended_float.astype(jnp.bfloat16).reshape(row_count, D)
    residual = tokens_float + jnp.dot(attended, output_full, preferred_element_type=jnp.float32)
    scale_two = norm_factor(residual)
    unit_two = residual * scale_two
    normed_two = (unit_two * gain_two.astype(jnp.float32)).astype(jnp.bfloat16)
    router_prob = jax.nn.softmax(
        jnp.dot(normed_two, router_full, preferred_element_type=jnp.float32), axis=-1
    )
    pick_hot = (
        expert_ids[:, :, None] == jnp.arange(experts, dtype=jnp.int32)[None, None, :]
    ).astype(jnp.float32)
    chosen = jnp.sum(pick_hot * router_prob[:, None, :], axis=2)
    chosen_total = jnp.sum(chosen, axis=1, keepdims=True)
    gate_shares = chosen / chosen_total
    hot_int = pick_hot.astype(jnp.int32).reshape(row_count * 2, experts)
    earlier = jnp.cumsum(hot_int, axis=0) - hot_int
    slot_number = jnp.sum(earlier * hot_int, axis=1).reshape(row_count, 2)
    kept_copy = slot_number < capacity
    kept_float = kept_copy.astype(jnp.float32)
    target = jnp.where(kept_copy, expert_ids * capacity + slot_number, experts * capacity)
    copy_ids = jnp.arange(row_count * 2, dtype=jnp.int32)
    slot_copy = (
        jnp.full((experts * capacity + 1,), row_count * 2, jnp.int32)
        .at[target.reshape(-1)]
        .set(copy_ids)[: experts * capacity]
    )
    fetch_index = jnp.minimum(target, experts * capacity - 1).reshape(-1)
    token_of_slot = jnp.where(slot_copy < row_count * 2, slot_copy // 2, row_count)
    padded = jnp.concatenate([normed_two, jnp.zeros((1, D), jnp.bfloat16)], axis=0)
    send_rows = padded[token_of_slot].reshape(experts, capacity, D)
    expert_in = lax.all_to_all(send_rows, EXPERT, split_axis=0, concat_axis=1, tiled=True)[0]
    gate_piece = lax.all_gather(gate_weight, SEQ, axis=1, tiled=True)
    up_piece = lax.all_gather(up_weight, SEQ, axis=1, tiled=True)
    down_piece = lax.all_gather(down_weight, SEQ, axis=1, tiled=True)
    gate_pre = jnp.einsum(SPEC_3, expert_in, gate_piece[0], preferred_element_type=jnp.float32)
    up_pre = jnp.einsum(SPEC_3, expert_in, up_piece[0], preferred_element_type=jnp.float32)
    active = (gelu_tanh(gate_pre) * up_pre).astype(jnp.bfloat16)
    expert_sum = jnp.dot(active, down_piece[0], preferred_element_type=jnp.float32)
    returned = lax.all_to_all(
        expert_sum.astype(jnp.bfloat16)[None], EXPERT, split_axis=1, concat_axis=0, tiled=True
    )
    picked = (
        returned.reshape(experts * capacity, D)[fetch_index]
        .reshape(row_count, 2, D)
        .astype(jnp.float32)
    )
    weighted = gate_shares * kept_float
    mixture = jnp.sum(weighted[:, :, None] * picked, axis=1)
    layer_out = (residual + mixture).astype(jnp.bfloat16)
    local_sums = jnp.stack([jnp.sum(residual * residual), jnp.sum(mixture * mixture)])
    again = (
        lax.all_gather(attention_gain, BOTH, axis=0, tiled=True),
        lax.all_gather(query_weight, BOTH, axis=0, tiled=True),
        lax.all_gather(key_weight, BOTH, axis=0, tiled=True),
        lax.all_gather(value_weight, BOTH, axis=0, tiled=True),
        lax.all_gather(output_weight, BOTH, axis=0, tiled=True),
        lax.all_gather(bias_table, BOTH, axis=0, tiled=True),
        lax.all_gather(feedforward_gain, BOTH, axis=0, tiled=True),
        lax.all_gather(router_weight, BOTH, axis=0, tiled=True),
    )
    gain_one, query_full, key_full, value_full, output_full, bias_flat, gain_two, router_full = (
        again
    )
    bias_grid = bias_flat.reshape(BUCKETS, HEADS)
    grad_out = cotangent.astype(jnp.float32)
    copy_grad = (
        (weighted[:, :, None] * grad_out[:, None, :]).astype(jnp.bfloat16).reshape(row_count * 2, D)
    )
    copy_padded = jnp.concatenate([copy_grad, jnp.zeros((1, D), jnp.bfloat16)], axis=0)
    grad_send = copy_padded[slot_copy].reshape(experts, capacity, D)
    grad_in = lax.all_to_all(grad_send, EXPERT, split_axis=0, concat_axis=1, tiled=True)[0]
    gate_piece = lax.all_gather(gate_weight, SEQ, axis=1, tiled=True)
    up_piece = lax.all_gather(up_weight, SEQ, axis=1, tiled=True)
    down_piece = lax.all_gather(down_weight, SEQ, axis=1, tiled=True)
    gate_pre = jnp.einsum(SPEC_3, expert_in, gate_piece[0], preferred_element_type=jnp.float32)
    up_pre = jnp.einsum(SPEC_3, expert_in, up_piece[0], preferred_element_type=jnp.float32)
    gelu_out, gelu_pull = jax.vjp(gelu_tanh, gate_pre)
    act_grad = jnp.einsum(SPEC_3, grad_in, down_piece[0], preferred_element_type=jnp.float32)
    gate_back = gelu_pull(act_grad * up_pre)[0].astype(jnp.bfloat16)
    up_back = (act_grad * gelu_out).astype(jnp.bfloat16)
    input_grad = jnp.dot(gate_back, gate_piece[0], preferred_element_type=jnp.float32) + jnp.dot(
        up_back, up_piece[0], preferred_element_type=jnp.float32
    )
    active = (gelu_out * up_pre).astype(jnp.bfloat16)
    input_grad, gate_backs, up_backs, actives = (input_grad, gate_back, up_back, active)
    grad_back = lax.all_to_all(
        input_grad.astype(jnp.bfloat16)[None], EXPERT, split_axis=1, concat_axis=0, tiled=True
    )
    expert_back = (
        grad_back.reshape(experts * capacity, D)[fetch_index]
        .reshape(row_count, 2, D)
        .astype(jnp.float32)
    )
    normed_two_grad = jnp.sum(expert_back * kept_float[:, :, None], axis=1)
    expert_grads = lax.psum_scatter(
        jnp.stack(
            [
                jnp.einsum(SPEC_4, gate_backs, expert_in, preferred_element_type=jnp.float32),
                jnp.einsum(SPEC_4, up_backs, expert_in, preferred_element_type=jnp.float32),
                jnp.einsum(SPEC_4, actives, grad_in, preferred_element_type=jnp.float32),
            ],
            axis=1,
        ).astype(jnp.bfloat16),
        SEQ,
        scatter_dimension=0,
        tiled=True,
    ).astype(jnp.float32)
    share_grad = jnp.sum(grad_out[:, None, :] * picked, axis=2) * kept_float
    chosen_grad = (
        share_grad - jnp.sum(gate_shares * share_grad, axis=1, keepdims=True)
    ) / chosen_total
    prob_grad = jnp.sum(pick_hot * chosen_grad[:, :, None], axis=1)
    logit_grad = router_prob * (prob_grad - jnp.sum(router_prob * prob_grad, axis=1, keepdims=True))
    router_float = router_full.astype(jnp.float32)
    router_term = jnp.einsum(
        SPEC_5, normed_two.astype(jnp.float32), logit_grad, precision=lax.Precision.HIGHEST
    )
    normed_two_grad = normed_two_grad + jnp.einsum(
        SPEC_6, logit_grad, router_float, precision=lax.Precision.HIGHEST
    )
    gain_two_term = jnp.sum(normed_two_grad * unit_two, axis=0)
    unit_grad_two = normed_two_grad * gain_two.astype(jnp.float32)
    residual_grad = grad_out + scale_two * (
        unit_grad_two - unit_two * jnp.mean(unit_grad_two * unit_two, axis=-1, keepdims=True)
    )
    attention_out_grad = residual_grad.astype(jnp.bfloat16)
    output_term = jnp.einsum(
        SPEC_5, attended, attention_out_grad, preferred_element_type=jnp.float32
    )
    attended_grad = (
        jnp.einsum(SPEC_6, attention_out_grad, output_full, preferred_element_type=jnp.float32)
        .astype(jnp.bfloat16)
        .reshape(row_count, HEADS, HDIM)
    )
    row_delta = jnp.transpose(jnp.sum(attended_grad.astype(jnp.float32) * attended_float, axis=-1))
    total_all, delta_all = (
        lax.all_gather(log_total, SEQ, axis=1, tiled=True),
        lax.all_gather(row_delta, SEQ, axis=1, tiled=True),
    )
    key_piece = lax.all_gather(keys_own, SEQ, axis=0, tiled=True)
    value_piece = lax.all_gather(values_own, SEQ, axis=0, tiled=True)
    key_rows = jnp.arange(key_piece.shape[0], dtype=jnp.int32)
    visible, onehot, pair_bias = pair_terms(
        own_meta, token_info(key_rows, starts, before, reaches), own_rows, key_rows, bias_grid
    )
    scores = masked_scores(queries, key_piece, visible, pair_bias)
    soft_weights = jnp.exp(scores - log_total[:, :, None])
    dprob = jnp.einsum(
        SPEC_1, attended_grad, value_piece, preferred_element_type=jnp.float32
    )
    score_grad = (soft_weights * (dprob - row_delta[:, :, None])).astype(jnp.bfloat16)
    query_acc = jnp.einsum(
        SPEC_2, score_grad, key_piece, preferred_element_type=jnp.float32
    )
    bias_acc = jnp.einsum(SPEC_7, onehot, score_grad, preferred_element_type=jnp.float32)
    query_acc, bias_acc = (query_acc, bias_acc)
    query_piece = lax.all_gather(queries, SEQ, axis=0, tiled=True)
    grad_piece = lax.all_gather(attended_grad, SEQ, axis=0, tiled=True)
    piece_rows = query_piece.shape[0]
    query_rows = jnp.arange(piece_rows, dtype=jnp.int32)
    visible, onehot, pair_bias = pair_terms(
        token_info(query_rows, starts, before, reaches), own_meta, query_rows, own_rows, bias_grid
    )
    scores = masked_scores(query_piece, keys_own, visible, pair_bias)
    soft_weights = jnp.exp(scores - total_all[:, :, None])
    value_acc = jnp.einsum(
        SPEC_8,
        soft_weights.astype(jnp.bfloat16),
        grad_piece,
        preferred_element_type=jnp.float32,
    )
    dprob = jnp.einsum(SPEC_1, grad_piece, values_own, preferred_element_type=jnp.float32)
    score_grad = (soft_weights * (dprob - delta_all[:, :, None])).astype(jnp.bfloat16)
    key_acc = jnp.einsum(
        SPEC_8, score_grad, query_piece, preferred_element_type=jnp.float32
    )
    key_acc, value_acc = (key_acc, value_acc)
    query_back = (query_acc * score_scale).astype(jnp.bfloat16).reshape(row_count, D)
    key_back = (key_acc * score_scale).astype(jnp.bfloat16).reshape(row_count, D)
    value_back = value_acc.astype(jnp.bfloat16).reshape(row_count, D)
    query_term = jnp.einsum(SPEC_5, normed_one, query_back, preferred_element_type=jnp.float32)
    key_term = jnp.einsum(SPEC_5, normed_one, key_back, preferred_element_type=jnp.float32)
    value_term = jnp.einsum(SPEC_5, normed_one, value_back, preferred_element_type=jnp.float32)
    normed_one_grad = jnp.einsum(
        SPEC_6, query_back, query_full, preferred_element_type=jnp.float32
    )
    normed_one_grad = normed_one_grad + jnp.einsum(
        SPEC_6, key_back, key_full, preferred_element_type=jnp.float32
    )
    normed_one_grad = normed_one_grad + jnp.einsum(
        SPEC_6, value_back, value_full, preferred_element_type=jnp.float32
    )
    gain_one_term = jnp.sum(normed_one_grad * unit_one, axis=0)
    unit_grad_one = normed_one_grad * gain_one.astype(jnp.float32)
    tokens_grad = residual_grad + scale_one * (
        unit_grad_one - unit_one * jnp.mean(unit_grad_one * unit_one, axis=-1, keepdims=True)
    )
    stats_term = jnp.broadcast_to(local_sums[None, :], (all_count, 2))
    reduced = (
        lax.psum_scatter(gain_one_term, BOTH, scatter_dimension=0, tiled=True),
        lax.psum_scatter(query_term, BOTH, scatter_dimension=0, tiled=True),
        lax.psum_scatter(key_term, BOTH, scatter_dimension=0, tiled=True),
        lax.psum_scatter(value_term, BOTH, scatter_dimension=0, tiled=True),
        lax.psum_scatter(output_term, BOTH, scatter_dimension=0, tiled=True),
        lax.psum_scatter(
            bias_acc.reshape(BUCKETS * HEADS), BOTH, scatter_dimension=0, tiled=True
        ),
        lax.psum_scatter(gain_two_term, BOTH, scatter_dimension=0, tiled=True),
        lax.psum_scatter(router_term, BOTH, scatter_dimension=0, tiled=True),
        lax.psum_scatter(stats_term, BOTH, scatter_dimension=0, tiled=True),
    )
    roots = jnp.sqrt(reduced[8][0] / (row_count * all_count * D))
    return (
        layer_out,
        tokens_grad,
        reduced[0],
        reduced[1],
        reduced[2],
        reduced[3],
        reduced[4],
        reduced[5],
        reduced[6],
        reduced[7],
        expert_grads[None, :, 0, :],
        expert_grads[None, :, 1, :],
        expert_grads[None, :, 2, :],
        roots,
    )


def solution(mesh):
    kernels_fit = mesh.shape[EXPERT] == len(ORDER) and mesh.shape[SEQ] == 4
    return jax.shard_map(
        per_device_kernels if kernels_fit else per_device_general,
        mesh=mesh,
        in_specs=(
            P(BOTH, None),
            P(BOTH, None),
            P(BOTH, None),
            P(EXPERT, None),
            P(EXPERT, None),
            P(BOTH),
            P(BOTH, None),
            P(BOTH, None),
            P(BOTH, None),
            P(BOTH, None),
            P(BOTH),
            P(BOTH),
            P(BOTH, None),
            P(EXPERT, SEQ, None),
            P(EXPERT, SEQ, None),
            P(EXPERT, SEQ, None),
        ),
        out_specs=(
            P(BOTH, None),
            P(BOTH, None),
            P(BOTH),
            P(BOTH, None),
            P(BOTH, None),
            P(BOTH, None),
            P(BOTH, None),
            P(BOTH),
            P(BOTH),
            P(BOTH, None),
            P(EXPERT, SEQ, None),
            P(EXPERT, SEQ, None),
            P(EXPERT, SEQ, None),
            P(),
        ),
        check_vma=False,
    )
```

profile of v0, /device:TPU:0, one launch (start us, length us, event | category | flops | bytes accessed | tf_op | source)
XLA Modules:
  0.0 303.9 jit_solution(13251896227548751124)
XLA Ops:
  0.6 68.7 %front.1 = (bf16[640,1024]{1,0:T(8,128)(2,1)}, bf16[640,1024]{1,0:T(8,128)(2,1)}, f32[8,8,128]{2,1,0:T(8,128)}, f32[256,1024]{1,0:T(8,128)}, bf16[1024,1024]{1,0...) custom-call(s32[1,13]{1,0:T(1,128)} %lengths.3, ...), custom_call_target="tpu_custom_call" | custom-call | flops 2684354560 | bytes 25165824 | tf_op jit(solution)/shard_map/front/pallas_call | solution.py:913
  69.4 130.1 %experts.1 = (bf16[4,2,4,80,1024]{4,3,2,1,0:T(8,128)(2,1)}, bf16[640,1024]{1,0:T(8,128)(2,1)}, f32[8,8,128]{2,1,0:T(8,128)}, bf16[704,1024]{1,0:T(8,128)(2,1)}, ...) custom-call(bf16[640,1024]{1,0:T(8,128)(2,1)} %get-tuple-element.54.xs, bf16[640,1024]{1,0:T(8,128)(2,1)} %get-tuple-element.55.gs, ...), custom_call_target="tpu_custom_call" | custom-call | flops 33218887680 | bytes 20971520 | tf_op jit(solution)/shard_map/experts/pallas_call | solution.py:436
  199.5 96.9 %back.1 = (bf16[256,1024]{1,0:T(8,128)(2,1)}, f32[256,1024]{1,0:T(8,128)}, f32[32,1024]{1,0:T(8,128)}, f32[32,1024]{1,0:T(8,128)}, f32[32,1024]{1,0:T(8,128)}, /*index=5*/f32[32,1024]{1,0:T(8,128)}, f32[16,1024]{1,0:T(8,128)}) custom-call(s32[1,13]{1,0:T(1,128)} %lengths.3, s32[1,13]{1,0:T(1,128)} %parents.3, s32[2,256]{1,0:T(2,128)} %bitcast.26, ...), custom_call_target="tpu_custom_call" | custom-call | flops 8053063680 | bytes 20971520 | tf_op jit(solution)/shard_map/back/pallas_call | solution.py:1432
  296.4 7.3 %emit.1 = (bf16[256,1024]{1,0:T(8,128)(2,1)}, f32[256,1024]{1,0:T(8,128)}, f32[32,1024]{1,0:T(8,128)}, f32[32,1024]{1,0:T(8,128)}, f32[32,1024]{1,0:T(8,128)}, /...) custom-call(bf16[256,1024]{1,0:T(8,128)(2,1)} %get-tuple-element.68., ...), custom_call_target="tpu_custom_call" | custom-call | tf_op jit(solution)/shard_map/emit/pallas_call | solution.py:1530
where the time goes:
time: 307 us; the launch traced here: 304 us
  Pallas kernels  303 us (99%)
    pallas_call x1, Pallas kernels, experts(): pl.pallas_call(expert_kernel, out_shape=(jax.ShapeDtypeStruct(part, low),...  130 us
    pallas_call x1, Pallas kernels, back(): pl.pallas_call(back_kernel, out_shape=(jax.ShapeDtypeStruct((rows, width)...  96.9 us
    pallas_call x1, Pallas kernels, front(): pl.pallas_call(front_kernel, out_shape=(jax.ShapeDtypeStruct((8 * cap, wi...  68.7 us
    pallas_call x1, Pallas kernels, emit(): pl.pallas_call(emit_kernel, out_shape=tuple((jax.ShapeDtypeStruct(x.shape...  7.33 us

commit v1 on v0

--- a/solution.py
+++ b/solution.py
@@ -123,11 +123,15 @@
 )
 
 
-def greet(peers):
+def announce(peers):
     barrier = pltpu.get_barrier_semaphore()
     for peer in peers:
         pl.semaphore_signal(barrier, inc=1, device_id=peer, device_id_type=MESH)
-    pl.semaphore_wait(barrier, len(peers))
+
+
+def greet(peers):
+    announce(peers)
+    pl.semaphore_wait(pltpu.get_barrier_semaphore(), len(peers))
 
 
 def aligned(index, size):
@@ -584,12 +588,12 @@
 
 def front_kernel(
     lengths, parents, tokens, cotangent, ids_row, wq, wk, wv, wo, gain_one, gain_two, bias, router_row,
-    xs, gs_far, shares, residual, all_tokens_far, qkv_far, cols_far, params, att_far, stats_far, wo_far, g_far,
-    all_tokens, qkv, cols, wo_full, att, stats, got, part, normed, misc, tags, tag_sum, all_tags, index, table, landed, gs, g_early,
+    xs, gs_far, shares, residual, all_tokens_far, qkv_far, cols_far, params, att_far, probs_far, wo_far, g_far,
+    all_tokens, qkv, cols, wo_full, att, probs, got, part, normed, misc, tags, tag_sum, all_tags, index, table, landed, gs, g_early,
     before_mem, reach_mem,
     t_send, t_recv, w_send, w_recv, m_send, m_recv, c_send, c_recv, n_send, n_recv,
     h_send, h_recv, a_send, a_recv,
-    e_send, e_recv, j_send, j_recv, far_sem,
+    e_send, e_recv, j_send, j_recv, far_sem, save_sem,
 ):
     e, s = lax.axis_index(EXPERT), lax.axis_index(SEQ)
     near_x, near_y, corner = (e, s ^ 1), (e, s ^ 2), (e, s ^ 3)
@@ -722,7 +726,6 @@
     g_early[0, 0] = gs[pl.ds(pl.multiple_of(e * cap, 16), cap), :]
     keep(gs, gs_far)
     found = segment_scalars(lengths, parents, before_mem, reach_mem)
-    stats[...] = jnp.zeros_like(stats)
     for r in range(4):
         index[r, :, :(r + 1) * rows] = pair_index(found, r * rows, rows, (r + 1) * rows)[0]
     for k in range(1, 4):
@@ -764,6 +767,10 @@
     lax.fori_loop(3, 4, norm_block, 0)
     keep(all_tokens, all_tokens_far)
 
+    def save_probs(p, r):
+        piece = probs.at[pl.ds(2 * p, 2), r, :, pl.ds(0, (r + 1) * rows)]
+        return pltpu.make_async_copy(piece, probs_far.at[pl.ds(2 * p, 2), r, :, pl.ds(0, (r + 1) * rows)], save_sem.at[p, r])
+
     def pair(p, carry):
         for which in range(2):
             @pl.when(p == which)
@@ -784,53 +791,51 @@
             v = qkv[p, 0:count, 256:384]
             lane = lax.broadcasted_iota(jnp.int32, (rows, 128), 1)
             results = []
-            noted = stats[first:count, :]
             for side in range(2):
                 mine = (lane // HDIM) == side
                 scores = contract(jnp.where(mine, q, jnp.zeros_like(q)), k, ((1,), (1,)))
                 scores = scores + looked_up(table[pl.ds(2 * p + side, 1), :], index[r, :, :count])
-                peak = jnp.max(scores, axis=1, keepdims=True)
-                expo = jnp.exp(scores - peak)
-                mass = jnp.sum(expo, axis=1, keepdims=True)
-                results.append(contract(expo.astype(low), v, ((1,), (0,))) * (1.0 / mass))
-                noted = jnp.where(lane == 2 * p + side, peak + jnp.log(mass), noted)
-            stats[first:count, :] = noted
+                expo = jnp.exp(scores - jnp.max(scores, axis=1, keepdims=True))
+                soft = (expo * (1.0 / jnp.sum(expo, axis=1, keepdims=True))).astype(low)
+                probs[2 * p + side, r, :, :count] = soft
+                results.append(contract(soft, v, ((1,), (0,))))
             att[first:count, aligned(p, 128)] = jnp.where((lane // HDIM) == 0, results[0], results[1]).astype(low)
+
+            save_probs(p, r).start()
 
             @pl.when((p == 1) & (s != r))
             def _():
                 give(r).start()
 
-            if r == 3:
+            if r == 2:
                 @pl.when(p == 0)
                 def _():
-                    g_corner(0)
                     for i in (2, 3):
                         g_entry(i).wait_recv()
                     for which in range(2):
                         g_hop(which, 1).start()
-
-                @pl.when(p == 1)
+            if r == 1:
+                @pl.when(p == 0)
                 def _():
-                    g_corner(1)
-            if r == 1:
+                    g_corner(0)
+                    for i in range(1, 4):
+                        share(i, 1).wait_recv()
+                        relay(i, 1).start()
+
                 @pl.when(p == 1)
                 def _():
                     for i in range(1, 4):
                         along_out(i).wait_recv()
                         relay_along(i).start()
-            if r == 1:
-                @pl.when(p == 0)
+            if r == 0:
+                @pl.when(p == 1)
                 def _():
-                    for i in range(1, 4):
-                        share(i, 1).wait_recv()
-                        relay(i, 1).start()
+                    g_corner(1)
         return carry
 
     lax.fori_loop(0, 2, pair, 0)
     keep(qkv, qkv_far)
     keep(cols, cols_far)
-    keep(stats, stats_far)
     along_out(0).wait_recv()
     for k in range(1, 4):
         relay_along(k).wait_recv()
@@ -892,6 +897,9 @@
             give(r).wait_send()
     for copy in far:
         copy.wait()
+    for p in range(2):
+        for r in range(4):
+            save_probs(p, r).wait()
 
 
 def front(lengths, parents, tokens, cotangent, ids_row, wq, wk, wv, wo, gain_one, gain_two, bias, router_row):
@@ -907,7 +915,7 @@
         jax.ShapeDtypeStruct((2, width, 3 * shard // 2), low),
         jax.ShapeDtypeStruct((16, width), full),
         jax.ShapeDtypeStruct((4, rows, shard), low),
-        jax.ShapeDtypeStruct((4 * rows, 128), full),
+        jax.ShapeDtypeStruct((4, 4, rows, 4 * rows), low),
         jax.ShapeDtypeStruct((8, 4, slim, width), low),
     )
     return pl.pallas_call(
@@ -922,7 +930,7 @@
         out_specs=(vmem, hbm, vmem, vmem, hbm, hbm, hbm, vmem, hbm, hbm, hbm, hbm),
         scratch_shapes=[
             pltpu.VMEM(kept[0].shape, low), pltpu.VMEM(kept[1].shape, low), pltpu.VMEM(kept[2].shape, low),
-            pltpu.VMEM(kept[6].shape, low), pltpu.VMEM((4 * rows, shard), low), pltpu.VMEM(kept[5].shape, full),
+            pltpu.VMEM(kept[6].shape, low), pltpu.VMEM((4 * rows, shard), low), pltpu.VMEM(kept[5].shape, low),
             pltpu.VMEM((3, 4 * slim, shard), low), pltpu.VMEM((2, 4 * slim, 3 * shard // 2), low),
             pltpu.VMEM((4 * rows, width), low),
             pltpu.VMEM((16, width), low), pltpu.VMEM((3, 16, width), low), pltpu.VMEM((16, width), low),
@@ -934,7 +942,7 @@
             dma((4,)), dma((4,)), dma((3, 3)), dma((3, 3)), dma((3,)), dma((3,)),
             dma((2, 7)), dma((2, 7)), dma((7,)), dma((7,)),
             dma((10,)), dma((10,)), dma((4,)), dma((4,)),
-            dma((4,)), dma((4,)), dma((4, 2)), dma((4, 2)), dma((8,)),
+            dma((4,)), dma((4,)), dma((4, 2)), dma((4, 2)), dma((8,)), dma((2, 4)),
         ],
         compiler_params=pltpu.CompilerParams(
             collective_id=2, has_side_effects=True, vmem_limit_bytes=VMEM_LIMIT
@@ -942,15 +950,6 @@
         cost_estimate=pl.CostEstimate(flops=40 * rows * width * shard, bytes_accessed=24 << 20, transcendentals=8 * rows * rows * 16),
         name="front",
     )(lengths, parents, tokens, cotangent, ids_row, wq, wk, wv, wo, gain_one, gain_two, bias, router_row)
-
-
-def pair_index_across(found, first, rows, count):
-    ids = first + lax.broadcasted_iota(jnp.int32, (1, rows), 1)
-    keys = lax.broadcasted_iota(jnp.int32, (count, 1), 0)
-    place, reach, _ = token_columns(found, ids)
-    key_place, _, key_own = token_columns(found, keys)
-    seen = ((reach & key_own) != 0) & (keys <= ids)
-    return jnp.where(seen, jnp.minimum(place - key_place, LAST - 1), LAST)
 
 
 def near_keys(found, first, rows):
@@ -970,14 +969,14 @@
 
 def back_kernel(
     lengths, parents, ids_row, params, ret_s, po_far, ret_b_far, residual_far, cotangent_far,
-    wo_far, qkv_far, cols_far, all_tokens_far, att_far, stats_far,
+    wo_far, qkv_far, cols_far, all_tokens_far, att_far, probs_far,
     layer_out_far, tokens_grad, dwq, dwk, dwv, dwo, small_sum,
-    po0, po2, ro, ro2, ret_o, ret_b, residual, cotangent, layer_out, wo, qkv, cols, all_tokens, att, stats, datt, datt_own, aog_own, residual_grad,
-    o_halves, o_core, o_sums, o_z, o_final, o_seq, index, spots, lse, table, near, dk, dv, dqkv, normed,
+    po0, po2, ro, ro2, ret_o, ret_b, residual, cotangent, layer_out, wo, qkv, cols, all_tokens, att, probs, datt, datt_own, aog_own, residual_grad,
+    takes, o_halves, o_core, o_sums, o_z, o_final, o_seq, spots, near, dk, dv, dqkv, normed,
     halves, core_got, sums, z_got, final, final_got, parts, first_got, second_got, mine, tally, tally_got, square, square_got,
     before_mem, reach_mem,
     load_sem, d_send, d_recv, w_send, w_recv, core_send, core_recv, z_send, z_recv, a_send, a_recv,
-    n_send, n_recv, m_send, m_recv, o_send, o_recv, r_send, r_recv, q_send, q_recv, own_sem,
+    n_send, n_recv, m_send, m_recv, o_send, o_recv, r_send, r_recv, q_send, q_recv, own_sem, probs_sem,
 ):
     e, s = lax.axis_index(EXPERT), lax.axis_index(SEQ)
     z, c = e // 2, lax.rem(e, 2)
@@ -993,13 +992,23 @@
     half = shard // 2
     pairs = (
         (residual_far, residual), (cotangent_far, cotangent), (ret_b_far, ret_b), (wo_far, wo), (po_far.at[0], po0),
-        (att_far, att), (stats_far, stats), (qkv_far, qkv), (all_tokens_far, all_tokens), (cols_far, cols),
+        (att_far, att), (qkv_far, qkv), (all_tokens_far, all_tokens), (cols_far, cols),
         (po_far.at[2, 0], po2.at[0]), (po_far.at[1, 1], po2.at[1]),
     )
     loads = [pltpu.make_async_copy(src, dst, load_sem.at[k]) for k, (src, dst) in enumerate(pairs)]
-    for load in loads:
+    for load in loads[:4]:
         load.start()
-    greet(around + [(e ^ d, s) for d in range(1, 8)])
+    peers = around + [(e ^ d, s) for d in range(1, 8)]
+    announce(peers)
+    early_probs = [
+        pltpu.make_async_copy(probs_far.at[:, r, :, pl.ds(0, (r + 1) * rows)], probs.at[:, r, :, pl.ds(0, (r + 1) * rows)],
+                              probs_sem.at[r])
+        for r in range(4)
+    ]
+    _, hot, slot, target, _ = slots_of(ids_row[...], cap)
+    place = lax.broadcasted_iota(jnp.int32, (rows, 8 * cap), 1)
+    takes[...] = jnp.where((place == target[0]) | (place == target[1]), 1.0, 0.0).astype(low)
+    pl.semaphore_wait(pltpu.get_barrier_semaphore(), len(peers))
 
     def o_copy(side, which, zone):
         first, second = ((near_x, near_y), (near_y, near_x))[side]
@@ -1017,10 +1026,9 @@
         return remote(po0.at[place % 2, place // 2], ret_o.at[block(e)], r_send.at[place], r_recv.at[place],
                       (e ^ ORDER[place], s))
 
-    def start_outs(zone):
-        for which in (1, 0):
-            for side in range(2):
-                o_copy(side, which, zone).start()
+    def start_outs(zone, which):
+        for side in range(2):
+            o_copy(side, which, zone).start()
 
     def add_outs(zone):
         for side in range(2):
@@ -1042,14 +1050,11 @@
                 else:
                     ret_o[block(e), :] = po0[0, 0]
 
-    start_outs(1)
+    start_outs(1, 1)
     loads[0].wait()
 
     held = residual[...]
-    _, hot, slot, target, _ = slots_of(ids_row[...], cap)
     scale, unit, unrouted, router, prob, chosen_sum, shares = router_of(held, params[...], hot)
-    place = lax.broadcasted_iota(jnp.int32, (rows, 8 * cap), 1)
-    takes = jnp.where((place == target[0]) | (place == target[1]), 1.0, 0.0).astype(low)
     at_slot = lax.broadcasted_iota(jnp.int32, (rows, 128), 1)
     dots = jnp.concatenate([ret_s[k, 0:1, :] for k in range(8)], axis=0)
     share_grad = []
@@ -1059,11 +1064,13 @@
             jnp.where((at_slot == slot[k]) & (slot[k] < cap), mine_dots, 0.0), axis=1, keepdims=True))
     for load in loads[1:4]:
         load.wait()
+    for load in loads[4:] + early_probs:
+        load.start()
     grad = cotangent[...].astype(full)
     inner = shares[0] * share_grad[0] + shares[1] * share_grad[1]
     prob_grad = sum(hot[k] * ((share_grad[k] - inner) / chosen_sum) for k in range(2))
     logit_grad = prob * (prob_grad - jnp.sum(prob * prob_grad, axis=1, keepdims=True))
-    normed_grad = contract(takes, ret_b[...], ((1,), (0,))) + lax.dot_general(
+    normed_grad = contract(takes[...], ret_b[...], ((1,), (0,))) + lax.dot_general(
         logit_grad, router, (((1,), (0,)), ((), ())), precision=high, preferred_element_type=full
     )
     unit_grad = normed_grad * params[1:2]
@@ -1083,7 +1090,13 @@
         return remote(o_halves.at[1 - c], o_core, w_send.at[0], w_recv.at[0], (e ^ 1, s))
 
     def wide_z(k):
-        return remote(o_sums.at[z ^ k], o_z.at[k - 1], w_send.at[k], w_recv.at[k], (e ^ (2 * k), s))
+        return remote(o_sums.at[z ^ (1, 3, 2)[k - 1]], o_z.at[k - 1], w_send.at[k], w_recv.at[k],
+                      (e ^ (2, 2, 4)[k - 1], s))
+
+    def wide_on():
+        wide_z(2).wait_recv()
+        o_sums[z ^ 2] = (o_sums[z ^ 2].astype(full) + o_z[1].astype(full)).astype(low)
+        wide_z(3).start()
 
     def wide_seq(k):
         return remote(o_final.at[aligned(s ^ (k + 1), slim)], o_seq.at[k], w_send.at[4 + k], w_recv.at[4 + k], around[k])
@@ -1109,17 +1122,12 @@
     wide_core().wait_recv()
     for j in range(4):
         o_sums[j] = (o_halves[c, j].astype(full) + o_core[j].astype(full)).astype(low)
-    for k in range(1, 4):
+    for k in (2, 1):
         wide_z(k).start()
     found = segment_scalars(lengths, parents, before_mem, reach_mem)
-    table[...] = bias_tables(params, s)
     near[...] = jnp.zeros_like(near)
     for r in range(4):
-        index[r, :(r + 1) * rows] = pair_index_across(found, r * rows, rows, (r + 1) * rows)
         spots[r] = near_keys(found, r * rows, rows)
-        turned = jnp.transpose(stats[r * rows:(r + 1) * rows, :])
-        for h in range(4):
-            lse[h, r] = turned[h:h + 1]
     gain = params[0:1]
 
     def units(q):
@@ -1170,9 +1178,12 @@
         for slot in range(first, first + amount):
             final_got[s, slot] = final[slot, aligned(s, slim)]
 
+    for load in early_probs:
+        load.wait()
     for k in range(3):
         give(k).wait_recv()
     add_outs(1)
+    start_outs(1, 0)
 
     def pair(p, carry):
         lanes = aligned(p, 128)
@@ -1194,18 +1205,16 @@
                 mine_lanes = (lane // HDIM) == side
                 q_side = jnp.where(mine_lanes, q, jnp.zeros_like(q))
                 g_side = jnp.where(mine_lanes, g, jnp.zeros_like(g))
-                scores = contract(k, q_side, ((1,), (1,)))
-                scores = scores + looked_up(table[pl.ds(2 * p + side, 1), :], index[r, :count])
-                soft = jnp.exp(scores - lse[2 * p + side, r])
-                dprob = contract(v, g_side, ((1,), (1,)))
-                delta = jnp.sum(soft * dprob, axis=0, keepdims=True)
-                turned = soft * (dprob - delta)
-                score_grad = turned.astype(low)
-                key_sum = key_sum + contract(score_grad, q_side, ((1,), (0,)))
-                value_sum = value_sum + contract(soft.astype(low), g_side, ((1,), (0,)))
-                wide = jnp.transpose(turned)
+                soft = probs[2 * p + side, r, :, :count]
+                wide_soft = soft.astype(full)
+                dprob = contract(g_side, v, ((1,), (1,)))
+                delta = jnp.sum(wide_soft * dprob, axis=1, keepdims=True)
+                wide = wide_soft * (dprob - delta)
+                score_grad = wide.astype(low)
+                key_sum = key_sum + contract(score_grad, q_side, ((0,), (0,)))
+                value_sum = value_sum + contract(soft, g_side, ((0,), (0,)))
                 with_ones = jnp.where((lane_long // HDIM) == side, k, jnp.ones_like(k))
-                part = contract(wide.astype(low), with_ones, ((1,), (0,)))
+                part = contract(score_grad, with_ones, ((1,), (0,)))
                 dq.append(part)
                 close = jnp.zeros((rows, 128), full)
                 for b in range(count // 128):
@@ -1221,12 +1230,17 @@
             if r == 3:
                 @pl.when(p == 0)
                 def _():
-                    finish_outs(1)
-                    start_outs(0)
+                    start_outs(0, 1)
+                    start_outs(0, 0)
+                    wide_on()
 
                 @pl.when(p == 1)
                 def _():
                     add_core(0)
+            if r == 2:
+                @pl.when(p == 0)
+                def _():
+                    finish_outs(1)
             if r == 1:
                 @pl.when(p == 1)
                 def _():
@@ -1288,11 +1302,9 @@
 
     lax.fori_loop(0, 4, back_block, 0)
     finish_outs(0)
-    for k in range(1, 4):
-        wide_z(k).wait_recv()
-    whole = o_sums[z].astype(full)
-    for k in range(3):
-        whole += o_z[k].astype(full)
+    wide_z(1).wait_recv()
+    wide_z(3).wait_recv()
+    whole = o_sums[z].astype(full) + o_z[0].astype(full) + o_z[2].astype(full)
     o_final[...] = whole.astype(low)
     for k in range(3):
         wide_seq(k).start()
@@ -1334,7 +1346,7 @@
 
     for place in range(1, 8):
         return_rows(place).wait_recv()
-    mixture = contract(takes, ret_o[...], ((1,), (0,)))
+    mixture = contract(takes[...], ret_o[...], ((1,), (0,)))
     layer_out[...] = (residual[...] + mixture).astype(low)
     layer_done = pltpu.make_async_copy(layer_out, layer_out_far, own_sem)
     layer_done.start()
@@ -1421,7 +1433,7 @@
                 o_copy(side, which, zone).wait_send()
 
 
-def back(lengths, parents, ids_row, params, ret_s, part_o, ret_b, residual, cotangent, wo, qkv, cols, all_tokens, att, stats):
+def back(lengths, parents, ids_row, params, ret_s, part_o, ret_b, residual, cotangent, wo, qkv, cols, all_tokens, att, probs):
     rows, width = residual.shape
     shard = att.shape[2]
     slim = width // 32
@@ -1443,14 +1455,14 @@
             pltpu.VMEM(ret_b.shape, low), pltpu.VMEM(ret_b.shape, low), pltpu.VMEM((rows, width), full),
             pltpu.VMEM((rows, width), low), pltpu.VMEM((rows, width), low),
             pltpu.VMEM((width, width), low), pltpu.VMEM(qkv.shape, low), pltpu.VMEM(cols.shape, low),
-            pltpu.VMEM(all_tokens.shape, low), pltpu.VMEM(att.shape, low), pltpu.VMEM(stats.shape, full),
+            pltpu.VMEM(all_tokens.shape, low), pltpu.VMEM(att.shape, low), pltpu.VMEM(probs.shape, low),
             pltpu.VMEM((4 * rows, shard), low), pltpu.VMEM((rows, width), low),
             pltpu.VMEM((rows, width), low), pltpu.VMEM((rows, width), full),
+            pltpu.VMEM((rows, ret_b.shape[0]), low),
             pltpu.VMEM((2, 4, half, width), low), pltpu.VMEM((4, half, width), low),
             pltpu.VMEM((4, half, width), low), pltpu.VMEM((3, half, width), low),
             pltpu.VMEM((half, width), low), pltpu.VMEM((3, slim, width), low),
-            pltpu.VMEM((4, 4 * rows, rows), jnp.int32), pltpu.VMEM((4, rows, 128), jnp.int32),
-            pltpu.VMEM((4, 4, 1, rows), full), pltpu.VMEM((8, 128), full), pltpu.VMEM((2, 8, 8, 128), full),
+            pltpu.VMEM((4, rows, 128), jnp.int32), pltpu.VMEM((2, 8, 8, 128), full),
             pltpu.VMEM((4 * rows, 128), full), pltpu.VMEM((4 * rows, 128), full),
             pltpu.VMEM((2, 4 * rows, 3 * shard // 2), low), pltpu.VMEM((4 * rows, width), low),
             pltpu.VMEM((2, 6, 4, half, half), low), pltpu.VMEM((6, 4, half, half), low),
@@ -1463,14 +1475,14 @@
             pltpu.SMEM((16,), jnp.int32), pltpu.SMEM((16,), jnp.int32),
             dma((12,)), dma((3,)), dma((3,)), dma((7,)), dma((7,)), dma((2,)), dma((2,)),
             dma((2, 3)), dma((2, 3)), dma((2, 3)), dma((2, 3)), dma((2, 3)), dma((2, 3)), dma((7,)), dma((7,)),
-            dma((2, 3, 2)), dma((2, 3, 2)), dma((8,)), dma((8,)), dma((7,)), dma((7,)), dma,
+            dma((2, 3, 2)), dma((2, 3, 2)), dma((8,)), dma((8,)), dma((7,)), dma((7,)), dma, dma((4,)),
         ],
         compiler_params=pltpu.CompilerParams(
             collective_id=5, has_side_effects=True, vmem_limit_bytes=VMEM_LIMIT
         ),
         cost_estimate=pl.CostEstimate(flops=120 * rows * width * shard, bytes_accessed=20 << 20, transcendentals=8 * rows * rows * 16),
         name="back",
-    )(lengths, parents, ids_row, params, ret_s, part_o, ret_b, residual, cotangent, wo, qkv, cols, all_tokens, att, stats)
+    )(lengths, parents, ids_row, params, ret_s, part_o, ret_b, residual, cotangent, wo, qkv, cols, all_tokens, att, probs)
 
 
 def emit_kernel(*refs):
@@ -1548,7 +1560,7 @@
     router_weight, gate_weight, up_weight, down_weight,
 ):
     ids_row = expert_ids.T
-    send_rows, grad_rows, shares, residual, all_tokens, qkv, cols, params, att, stats, wo, g_early = front(
+    send_rows, grad_rows, shares, residual, all_tokens, qkv, cols, params, att, probs, wo, g_early = front(
         segment_lengths, segment_parents, tokens, cotangent, ids_row, query_weight, key_weight, value_weight,
         output_weight, attention_gain[None], feedforward_gain[None], bias_table[None], router_weight.T,
     )
@@ -1557,7 +1569,7 @@
     )
     layer_out, tokens_grad, dwq, dwk, dwv, dwo, totals = back(
         segment_lengths, segment_parents, ids_row, params, dots, part_out, grad_back, residual, cotangent,
-        wo.reshape(D, D), qkv, cols, all_tokens, att, stats,
+        wo.reshape(D, D), qkv, cols, all_tokens, att, probs,
     )
     large = (layer_out, tokens_grad, dwq, dwk, dwv, dwo, gate_term, up_term, down_term)
     *large, gain_one, gain_two, bias, router, roots = emit(large, totals)

time: 307 us -> 306 us (level)
    pallas_call x1, Pallas kernels: 96.9 us -> 93.2 us  [back(): pl.pallas_call(back_kernel, out_shape=(jax.ShapeDtypeStruct((rows, width)...]
where the time goes in v1:
time: 306 us; the launch traced here: 302 us
  Pallas kernels  301 us (98%)
    pallas_call x1, Pallas kernels, experts(): pl.pallas_call(expert_kernel, out_shape=(jax.ShapeDtypeStruct(part, low),...  130 us
    pallas_call x1, Pallas kernels, back(): pl.pallas_call(back_kernel, out_shape=(jax.ShapeDtypeStruct((rows, width)...  93.2 us
    pallas_call x1, Pallas kernels, front(): pl.pallas_call(front_kernel, out_shape=(jax.ShapeDtypeStruct((8 * cap, wi...  70.8 us
    pallas_call x1, Pallas kernels, emit(): pl.pallas_call(emit_kernel, out_shape=tuple((jax.ShapeDtypeStruct(x.shape...  7.33 us

profile of v1, /device:TPU:0, one launch (start us, length us, event | category | flops | bytes accessed | tf_op | source)
XLA Modules:
  0.0 302.2 jit_solution(8494181724955770788)
XLA Ops:
  0.6 70.8 %front.1 = (bf16[640,1024]{1,0:T(8,128)(2,1)}, bf16[640,1024]{1,0:T(8,128)(2,1)}, f32[8,8,128]{2,1,0:T(8,128)}, f32[256,1024]{1,0:T(8,128)}, bf16[1024,1024]{1,0...) custom-call(s32[1,13]{1,0:T(1,128)} %lengths.3, ...), custom_call_target="tpu_custom_call" | custom-call | flops 2684354560 | bytes 25165824 | tf_op jit(solution)/shard_map/front/pallas_call | solution.py:921
  71.5 129.9 %experts.1 = (bf16[4,2,4,80,1024]{4,3,2,1,0:T(8,128)(2,1)}, bf16[640,1024]{1,0:T(8,128)(2,1)}, f32[8,8,128]{2,1,0:T(8,128)}, bf16[704,1024]{1,0:T(8,128)(2,1)}, ...) custom-call(bf16[640,1024]{1,0:T(8,128)(2,1)} %get-tuple-element.54.xs, bf16[640,1024]{1,0:T(8,128)(2,1)} %get-tuple-element.55.gs, ...), custom_call_target="tpu_custom_call" | custom-call | flops 33218887680 | bytes 20971520 | tf_op jit(solution)/shard_map/experts/pallas_call | solution.py:440
  201.4 93.2 %back.1 = (bf16[256,1024]{1,0:T(8,128)(2,1)}, f32[256,1024]{1,0:T(8,128)}, f32[32,1024]{1,0:T(8,128)}, f32[32,1024]{1,0:T(8,128)}, f32[32,1024]{1,0:T(8,128)}, /*index=5*/f32[32,1024]{1,0:T(8,128)}, f32[16,1024]{1,0:T(8,128)}) custom-call(s32[1,13]{1,0:T(1,128)} %lengths.3, s32[1,13]{1,0:T(1,128)} %parents.3, s32[2,256]{1,0:T(2,128)} %bitcast.26, ...), custom_call_target="tpu_custom_call" | custom-call | flops 8053063680 | bytes 20971520 | tf_op jit(solution)/shard_map/back/pallas_call | solution.py:1444
  294.6 7.3 %emit.1 = (bf16[256,1024]{1,0:T(8,128)(2,1)}, f32[256,1024]{1,0:T(8,128)}, f32[32,1024]{1,0:T(8,128)}, f32[32,1024]{1,0:T(8,128)}, f32[32,1024]{1,0:T(8,128)}, /...) custom-call(bf16[256,1024]{1,0:T(8,128)(2,1)} %get-tuple-element.68., ...), custom_call_target="tpu_custom_call" | custom-call | tf_op jit(solution)/shard_map/emit/pallas_call | solution.py:1542

commit v2 on v1

--- a/solution.py
+++ b/solution.py
@@ -384,8 +384,8 @@
         done.start()
         return done
 
+    finish(2)
     done = grads(gb, xr, dwg)
-    finish(2)
     add_second(3)
     start_sums(0)
     for q in range(1, 4):

time: 306 us -> 301 us (0.984)
  Pallas kernels: 301 us -> 297 us
where the time goes in v2:
time: 301 us; the launch traced here: 298 us
  Pallas kernels  297 us (99%)
    pallas_call x1, Pallas kernels, experts(): pl.pallas_call(expert_kernel, out_shape=(jax.ShapeDtypeStruct(part, low),...  128 us
    pallas_call x1, Pallas kernels, back(): pl.pallas_call(back_kernel, out_shape=(jax.ShapeDtypeStruct((rows, width)...  91.1 us
    pallas_call x1, Pallas kernels, front(): pl.pallas_call(front_kernel, out_shape=(jax.ShapeDtypeStruct((8 * cap, wi...  70.8 us
    pallas_call x1, Pallas kernels, emit(): pl.pallas_call(emit_kernel, out_shape=tuple((jax.ShapeDtypeStruct(x.shape...  7.33 us

profile of v2, /device:TPU:0, one launch (start us, length us, event | category | flops | bytes accessed | tf_op | source)
XLA Modules:
  0.0 297.8 jit_solution(12404204133570776881)
XLA Ops:
  0.6 70.8 %front.1 = (bf16[640,1024]{1,0:T(8,128)(2,1)}, bf16[640,1024]{1,0:T(8,128)(2,1)}, f32[8,8,128]{2,1,0:T(8,128)}, f32[256,1024]{1,0:T(8,128)}, bf16[1024,1024]{1,0...) custom-call(s32[1,13]{1,0:T(1,128)} %lengths.3, ...), custom_call_target="tpu_custom_call" | custom-call | flops 2684354560 | bytes 25165824 | tf_op jit(solution)/shard_map/front/pallas_call | solution.py:921
  71.5 127.6 %experts.1 = (bf16[4,2,4,80,1024]{4,3,2,1,0:T(8,128)(2,1)}, bf16[640,1024]{1,0:T(8,128)(2,1)}, f32[8,8,128]{2,1,0:T(8,128)}, bf16[704,1024]{1,0:T(8,128)(2,1)}, ...) custom-call(bf16[640,1024]{1,0:T(8,128)(2,1)} %get-tuple-element.54.xs, bf16[640,1024]{1,0:T(8,128)(2,1)} %get-tuple-element.55.gs, ...), custom_call_target="tpu_custom_call" | custom-call | flops 33218887680 | bytes 20971520 | tf_op jit(solution)/shard_map/experts/pallas_call | solution.py:440
  199.1 91.1 %back.1 = (bf16[256,1024]{1,0:T(8,128)(2,1)}, f32[256,1024]{1,0:T(8,128)}, f32[32,1024]{1,0:T(8,128)}, f32[32,1024]{1,0:T(8,128)}, f32[32,1024]{1,0:T(8,128)}, /*index=5*/f32[32,1024]{1,0:T(8,128)}, f32[16,1024]{1,0:T(8,128)}) custom-call(s32[1,13]{1,0:T(1,128)} %lengths.3, s32[1,13]{1,0:T(1,128)} %parents.3, s32[2,256]{1,0:T(2,128)} %bitcast.26, ...), custom_call_target="tpu_custom_call" | custom-call | flops 8053063680 | bytes 20971520 | tf_op jit(solution)/shard_map/back/pallas_call | solution.py:1444
  290.2 7.3 %emit.1 = (bf16[256,1024]{1,0:T(8,128)(2,1)}, f32[256,1024]{1,0:T(8,128)}, f32[32,1024]{1,0:T(8,128)}, f32[32,1024]{1,0:T(8,128)}, f32[32,1024]{1,0:T(8,128)}, /...) custom-call(bf16[256,1024]{1,0:T(8,128)(2,1)} %get-tuple-element.68., ...), custom_call_target="tpu_custom_call" | custom-call | tf_op jit(solution)/shard_map/emit/pallas_call | solution.py:1542
